TPU v7x, 512 devices: a whole 4x8x8 slice. The times are simulated.
512 devices in a mesh: pair: 64 (over z, y), ka: 8 (over x, core).
Axes of the slice: x: 4, y: 8, z: 8, core: 2. Of those that a mesh axis runs over, the one named last changes fastest.
Arguments:
- amplitude: bfloat16 [24576, 128, 128], P(('pair', 'ka')), may hold values from -6 to 6
- slot_owner: int32 [24576], P(('pair', 'ka')), may hold values from 0 to 63, as said below
- slot_tile: int32 [24576], P(('pair', 'ka')), may hold values from 0 to 2
- integrals: bfloat16 [1536, 128, 256], P(('pair', 'ka')), may hold values from -0.109375 to 0.109375
- tile_mask: int32 [1536, 2], P(('pair', 'ka')), may hold values 0 or 1
Outputs:
- residual: float32 [8192, 256], P(('pair', 'ka'))
Inputs may be any that keep to these rules, and one draw needn't show every extreme that they name: Among the 48 amplitude tiles of one device no two have the same slot_owner and slot_tile together.
All inputs are finite; a program needn't handle non-finite values. No bound on the sum of `tile_mask` on one device may be relied on, other than what follows from the above.
Results may differ from a plain program's by a relative error of at most 0.0003.
Values may be sent and summed in bfloat16 or wider, within the bound.
A program may use at most 64 MiB of HBM per device.

v0:
```python
import jax
import jax.numpy as jnp
from jax import lax
from jax.sharding import PartitionSpec as P


def local(amplitude, slot_owner, slot_tile, integrals, tile_mask):
    owner_count = lax.axis_size("pair")
    held_tiles, tile_edge, columns = integrals.shape
    band_count = columns // tile_edge
    masked = (
        integrals.reshape(held_tiles, tile_edge, band_count, tile_edge)
        * tile_mask.astype(jnp.bfloat16)[:, None, :, None]
    ).reshape(held_tiles, tile_edge, columns)
    targets = slot_owner * held_tiles + slot_tile
    candidate = jnp.arange(owner_count * held_tiles, dtype=jnp.int32)
    matches = targets[None, :] == candidate[:, None]
    positions = jnp.arange(targets.shape[0], dtype=jnp.int32)
    chosen = jnp.sum(jnp.where(matches, positions[None, :], 0), axis=1)
    present = jnp.any(matches, axis=1)
    picked = jnp.take(amplitude, chosen, axis=0)
    panels = jnp.where(present[:, None, None], picked, jnp.zeros((), jnp.bfloat16)).reshape(
        owner_count, held_tiles, tile_edge, tile_edge
    )
    partial_value = jnp.einsum(
        "pcij,cjk->pik",
        lax.all_to_all(panels, "pair", split_axis=0, concat_axis=0, tiled=True),
        masked,
        preferred_element_type=jnp.float32,
    )
    returned = lax.all_to_all(partial_value, "pair", split_axis=0, concat_axis=0, tiled=True)
    residual = jnp.sum(returned, axis=0)
    return lax.psum_scatter(residual, "ka", scatter_dimension=0, tiled=True)


def solution(mesh):
    in_specs = (
        P(("pair", "ka"), None, None),
        P(("pair", "ka")),
        P(("pair", "ka")),
        P(("pair", "ka"), None, None),
        P(("pair", "ka"), None),
    )
    out_specs = P(("pair", "ka"), None)
    return jax.shard_map(local, mesh=mesh, in_specs=in_specs, out_specs=out_specs, check_vma=False)
```

profile of v0, /device:TPU:1, one launch (start us, length us, event | category | flops | bytes accessed | tf_op | source)
XLA Modules:
  0.0 509.0 jit_solution(17203063968365428879)
XLA Ops:
  6.5 0.0 copy-start
  6.5 0.8 multiply_add_fusion
  7.3 0.1 fusion.3
  7.4 0.1 select_reduce_fusion
  7.5 0.1 reduce_sum.23
  7.7 0.1 broadcast_in_dim.41
  7.9 0.1 copy-done
  8.0 7.9 %gather_fusion = bf16[192,128,128]{2,1,0:T(8,128)(2,1)} fusion(bf16[48,128,128]{2,1,0:T(8,128)(2,1)S(1)} %copy-done, s32[1024]{0:T(1024)S(1)} %pad_clamp_fusion), kind=kCustom, calls=%fused_computation | custom fusion | bytes 12583680 | tf_op jit(solution)/shard_map/jit(_take)/gather | solution.py:21
  15.9 6.7 %select_select_fusion = bf16[64,3,128,128]{3,2,1,0:T(8,128)(2,1)} fusion(bf16[64,3,128,128]{3,2,1,0:T(8,128)(2,1)} %bitcast.15, pred[64,3]{1,0:T(8,128)(4,1)S(1)} %compare_and_fusion, pred[64,3]{1,0:T(8,128)(4,1)S(1)} %broadcast_in_dim.41), kind=kLoop, calls=%fused_computation.1 | loop fusion | flops 6291456 | bytes 12583296 | tf_op jit(solution)/shard_map/jit(_where)/select_n | solution.py:22
  22.6 0.0 copy-start.2
  22.6 0.0 copy-start.1
  22.6 17.5 %all-to-all-start = ((bf16[64,3,128,128]{3,2,1,0:T(8,128)(2,1)}), bf16[64,3,128,128]{3,2,1,0:T(8,128)(2,1)}, u32[]{:S(2)}, u32[]{:S(2)}) async-start(bf16[64,3,128,128]{3,2,1,0:T(8,128)(2,1)} %select_select_fusion), calls=%async_computation | async-start | bytes 12582912 | tf_op jit(solution)/shard_map/all_to_all | solution.py:27
  40.1 0.0 reduce-scatter.2.cloned.1.call-start
  40.2 0.0 copy-done.2
  40.2 0.1 copy.8
  40.3 0.1 broadcast_bitcast_fusion
  40.4 168.5 %all-to-all-done = bf16[64,3,128,128]{3,2,1,0:T(8,128)(2,1)} async-done(((bf16[64,3,128,128]{3,2,1,0:T(8,128)(2,1)}), bf16[64,3,128,128]{3,2,1,0:T(8,128)(2,1)}, u32[]{:S(2)}, u32[]{:S(2)}) %all-to-all-start) | async-done | bytes 6291488 | tf_op jit(solution)/shard_map/all_to_all | solution.py:27
  208.9 0.0 copy-done.1
  208.9 4.5 convolution_bitcast_fusion
  213.3 239.0 %all_to_all.10 = f32[64,128,256]{2,1,0:T(8,128)} all-to-all(f32[64,128,256]{2,1,0:T(8,128)S(1)} %convolution_bitcast_fusion), channel_id=1, replica_groups=mesh['pair'=64,'ka'=8] {'pair'}, dimensions={0} | all-to-all | bytes 16777216 | tf_op jit(solution)/shard_map/all_to_all | solution.py:31
  452.3 4.5 reduce_sum.25
  456.8 0.0 reduce-scatter.2.cloned.1.call-update
  456.9 45.3 %reduce-scatter.2.cloned.1.call-done = f32[16,256]{1,0:T(8,128)} async-done(((f32[128,256]{1,0:T(8,128)}), f32[16,256]{1,0:T(8,128)}) %reduce-scatter.2.cloned.1.call-update) | async-done | bytes 16400 | tf_op jit(solution)/shard_map/reduce_scatter | solution.py:33
  (5 shorter events, 0.0 us)
Async XLA Ops:
  6.5 1.4 copy-start
  22.6 17.6 %copy-start.2 = (s32[3,2]{0,1:T(2,128)S(1)}, s32[3,2]{0,1:T(2,128)}, u32[]{:S(2)}) copy-start(s32[3,2]{0,1:T(2,128)} %param.9) | copy-start | bytes 76
  22.6 186.2 %copy-start.1 = (bf16[3,128,256]{2,1,0:T(8,128)(2,1)S(1)}, bf16[3,128,256]{2,1,0:T(8,128)(2,1)}, u32[]{:S(2)}) copy-start(bf16[3,128,256]{2,1,0:T(8,128)(2,1)} %param.8) | copy-start | bytes 589828
  22.6 186.2 %all-to-all-start = ((bf16[64,3,128,128]{3,2,1,0:T(8,128)(2,1)}), bf16[64,3,128,128]{3,2,1,0:T(8,128)(2,1)}, u32[]{:S(2)}, u32[]{:S(2)}) async-start(bf16[64,3,128,128]{3,2,1,0:T(8,128)(2,1)} %select_select_fusion), calls=%async_computation | async-start | bytes 12582912 | tf_op jit(solution)/shard_map/all_to_all | solution.py:27
  40.1 462.0 %reduce-scatter.2.cloned.1.call-start = ((), (), s32[]{:S(2)}) async-start(), calls=%async_computation.3 | async-start | bytes 147456 | tf_op jit(solution)/shard_map/reduce_scatter | solution.py:33
Sparse Core Ops, SparseCore 0:
  457.0 45.1 reduce-scatter.1
where the time goes:
time: 510 us; the launch traced here: 509 us
  blocking collectives  239 us (47%)
  waiting for transfers between devices  214 us (42%)
  starting transfers between devices  17.5 us (3%)
  between operations  13.5 us (3%)
  other arithmetic  12.3 us (2%)
  local copies, waits for them, and re-layouts  8.51 us (2%)
    all_to_all x1, blocking collectives, local(): lax.all_to_all(partial_value, 'pair', split_axis=0, concat_axis=0, tiled=...  239 us
    all_to_all x1, waiting for transfers between devices, local(): lax.all_to_all(panels, 'pair', split_axis=0, concat_axis=0, tiled=True)  168 us
    reduce_scatter x1, waiting for transfers between devices, local(): return lax.psum_scatter(residual, 'ka', scatter_dimension=0, tiled=True)  45.3 us
    all_to_all x1, starting transfers between devices, local(): lax.all_to_all(panels, 'pair', split_axis=0, concat_axis=0, tiled=True)  17.5 us
  transfers between devices with their start and end apart: 2, of which 2 were waited for; matrix products, arithmetic and copies ran while one was open for 0% of the time, Pallas kernels for 0%

commit v1 on v0

v1 whole, which is shorter than its diff:
```python
import functools

import jax
import jax.numpy as jnp
from jax import lax
from jax.experimental import pallas as pl
from jax.experimental.pallas import tpu as pltpu
from jax.sharding import PartitionSpec as P

MESH = pl.DeviceIdType.MESH

TILE = 128
AB = 2
HELD = 3
NS = 48
RING = 8
KA = 8
MINE = HELD * AB
GROUP = RING * MINE
HALF = MINE // 2
ROWS = TILE // KA

CAPS = (30, 28, 24, 12)
HOPS = len(CAPS)
CUTS = (0,) + CAPS[::-1]


def region(sign, hop):
    return GROUP + sign * sum(CAPS) + sum(CAPS[: hop - 1])


ZERO_SLOT = GROUP + 2 * sum(CAPS)
SLOTS = ZERO_SLOT + 1


def kernel(
    owner_ref, tile_ref, mask_ref, integrals_ref, amplitude_ref,
    out_ref, flag_ref,
    amp, group, lists, pool, need_tx, need_rx, mask_rx, order, tab_tx, tab_rx, vote_tx, vote_rx,
    order_s, tab_s, index_s, total, part_tx, part_rx,
    local_sem, one_send, one_recv, two_send, two_recv, need_send, need_recv, mask_send, mask_recv,
    tab_send, tab_recv, vote_send, vote_recv, part_send, part_recv,
):
    pair, ka = lax.axis_index("pair"), lax.axis_index("ka")
    core = lax.rem(ka, 2)
    high, low = lax.div(pair, RING), lax.rem(pair, RING)
    u = high + core * (low - high)
    v = low + core * (high - low)
    stride_u, stride_v = RING - (RING - 1) * core, 1 + (RING - 1) * core

    def on_first(step):
        return (lax.rem(u + step + RING, RING) * stride_u + v * stride_v, ka)

    def on_second(step):
        return (u * stride_u + lax.rem(v + step + RING, RING) * stride_v, ka)

    def on_ka(step):
        return (pair, lax.rem(ka + step, KA))

    barrier = pltpu.get_barrier_semaphore()
    for step in range(1, RING):
        for there in (on_first(step), on_second(step), on_ka(step)):
            pl.semaphore_signal(barrier, inc=1, device_id=there, device_id_type=MESH)

    amp_copy = pltpu.make_async_copy(amplitude_ref, amp, local_sem.at[0])
    amp_copy.start()

    for t in range(HELD):
        for a in range(AB):
            block = integrals_ref[t, :, a * TILE : (a + 1) * TILE].astype(jnp.float32)
            scale = mask_ref[t, a].astype(jnp.float32)
            group[u * MINE + t * AB + a] = (block * scale).astype(jnp.bfloat16)

    lane = lax.broadcasted_iota(jnp.int32, (8, TILE), 1)
    own_mask = jnp.zeros((8, TILE), jnp.float32)
    for t in range(HELD):
        for a in range(AB):
            here = lane == u * MINE + t * AB + a
            own_mask = jnp.where(here, mask_ref[t, a].astype(jnp.float32), own_mask)
    mask_rx[0] = own_mask

    def source_of(s):
        owner = owner_ref[s]
        oh, ol = owner // RING, lax.rem(owner, RING)
        return oh + core * (ol - oh), ol + core * (oh - ol), tile_ref[s]

    code = lax.broadcasted_iota(jnp.int32, (RING, 8, TILE), 0) * TILE + lax.broadcasted_iota(
        jnp.int32, (RING, 8, TILE), 2
    ) // AB

    def mark(s, seen):
        su, sv, st = source_of(s)
        distance = lax.rem(sv - v + RING, RING)
        return jnp.where(code == distance * TILE + su * HELD + st, 1.0, seen)

    need_tx[...] = lax.fori_loop(0, NS, mark, jnp.zeros((RING, 8, TILE), jnp.float32))

    pool[ZERO_SLOT] = jnp.zeros((TILE, TILE), jnp.bfloat16)

    pl.semaphore_wait(barrier, 3 * (RING - 1))

    def remote(src, dst, send, recv, there):
        return pltpu.make_async_remote_copy(
            src_ref=src, dst_ref=dst, send_sem=send, recv_sem=recv, device_id=there, device_id_type=MESH
        )

    def first(sign, hop, chunk):
        behind = lax.rem(u + (hop - 1 if sign else RING - hop + 1), RING)
        ref = group.at[pl.ds(behind * MINE + chunk * HALF, HALF)]
        number = (sign * 4 + hop - 1) * 2 + chunk
        return remote(ref, ref, one_send.at[number], one_recv.at[number], on_first(-1 if sign else 1))

    def first_arrival(sign, hop, chunk):
        behind = lax.rem(u + (hop if sign else RING - hop), RING)
        ref = group.at[pl.ds(behind * MINE + chunk * HALF, HALF)]
        number = (sign * 4 + hop - 1) * 2 + chunk
        return remote(ref, ref, one_send.at[number], one_recv.at[number], on_first(-1 if sign else 1))

    need_copies = [
        remote(need_tx.at[j], need_rx.at[j], need_send.at[j], need_recv.at[j], on_second(j)) for j in range(1, RING)
    ]
    mask_copies = [
        remote(mask_rx.at[0], mask_rx.at[j], mask_send.at[j], mask_recv.at[j], on_first(j)) for j in range(1, RING)
    ]
    sent = []

    def start(copy):
        copy.start()
        sent.append(copy)

    for sign in range(2):
        start(first(sign, 1, 0))
    for copy in need_copies + mask_copies:
        start(copy)
    for sign in range(2):
        start(first(sign, 1, 1))
    for hop in (2, 3):
        for chunk in range(2):
            for sign in range(2):
                first_arrival(sign, hop - 1, chunk).wait_recv()
                start(first(sign, hop, chunk))

    for copy in need_copies + mask_copies:
        copy.wait_recv()
    mask = mask_rx[0]
    for j in range(1, RING):
        mask = jnp.maximum(mask, mask_rx[j])
    even = (lane % 2) == 0
    flane = lane.astype(jnp.float32)
    wide_lane = lax.broadcasted_iota(jnp.int32, (GROUP, TILE), 1)
    wide_row = lax.broadcasted_iota(jnp.int32, (GROUP, TILE), 0)
    ranks = []
    over = jnp.zeros((8, TILE), jnp.float32)
    for sign in range(2):
        far = jnp.zeros((8, TILE), jnp.float32)
        for distance in range(1, HOPS + 1):
            needed = need_rx[distance if sign else RING - distance] * mask
            if distance == HOPS:
                needed = jnp.where(even == (sign == 0), needed, 0.0)
            far = jnp.where(needed > 0.0, float(distance), far)
        for hop in range(1, HOPS + 1):
            count = jnp.sum(jnp.where(far >= float(hop), 1.0, 0.0), axis=1, keepdims=True)
            over = jnp.maximum(over, jnp.where(count > float(CAPS[hop - 1]), 1.0, 0.0))
        key = far * float(TILE) + (float(TILE - 1) - flane)
        key_row = jnp.broadcast_to(key[0:1], (GROUP, TILE))
        key_col = jnp.sum(jnp.where(wide_lane == wide_row, key_row, 0.0), axis=1, keepdims=True)
        rank_row = jnp.sum(jnp.where(key_col > key_row, 1.0, 0.0), axis=0, keepdims=True)
        rank_col = jnp.sum(jnp.where(key_row > key_col, 1.0, 0.0), axis=1, keepdims=True)
        chosen = jnp.where(rank_col == wide_lane.astype(jnp.float32), wide_row.astype(jnp.float32), 0.0)
        inverse = jnp.sum(chosen, axis=0, keepdims=True)
        order[sign] = jnp.broadcast_to(inverse, (8, TILE)).astype(jnp.int32)
        ranks.append(jnp.broadcast_to(rank_row, (8, TILE)))
    order_copy = pltpu.make_async_copy(order, order_s, local_sem.at[1])
    order_copy.start()

    sub = lax.broadcasted_iota(jnp.int32, (8, TILE), 0)
    for j in range(1, RING):
        right = ranks[0] + float(region(0, min(j, HOPS)))
        left = ranks[1] + float(region(1, min(RING - j, HOPS)))
        slot = right if j < HOPS else left if j > HOPS else jnp.where(even, right, left)
        slot = jnp.where(mask > 0.0, slot, float(ZERO_SLOT))
        tab_tx[j] = jnp.where(sub == 0, slot, over).astype(jnp.int32)
    tab_copies = [
        remote(tab_tx.at[j], tab_rx.at[j], tab_send.at[j], tab_recv.at[j], on_second(j)) for j in range(1, RING)
    ]
    tab_rx[0] = jnp.where(sub == 0, lane, over.astype(jnp.int32))

    for sign in range(2):
        first_arrival(sign, 3, sign).wait_recv()
        start(first(sign, 4, sign))
    for sign in range(2):
        first_arrival(sign, 3, 1 - sign).wait_recv()
    for copy in tab_copies:
        start(copy)
    order_copy.wait()
    for sign in range(2):
        first_arrival(sign, 4, sign).wait_recv()

    def second(sign, hop, piece):
        begin, size = CUTS[piece], CUTS[piece + 1] - CUTS[piece]
        if hop == 1:
            src = lists.at[sign, pl.ds(begin, size)]
        else:
            src = pool.at[pl.ds(region(sign, hop - 1) + begin, size)]
        dst = pool.at[pl.ds(region(sign, hop) + begin, size)]
        number = (sign * HOPS + hop - 1) * HOPS + piece
        return remote(src, dst, two_send.at[number], two_recv.at[number], on_second(-1 if sign else 1))

    for piece in range(HOPS):
        for sign in range(2):

            def pick(r, carry, sign=sign):
                lists[sign, r] = group[jnp.clip(order_s[sign, 0, r], 0, GROUP - 1)]
                return carry

            lax.fori_loop(CUTS[piece], CUTS[piece + 1], pick, 0)
            start(second(sign, 1, piece))
    own_copy = pltpu.make_async_copy(group, pool.at[pl.ds(0, GROUP)], local_sem.at[2])
    own_copy.start()

    for copy in tab_copies:
        copy.wait_recv()
    tab_copy = pltpu.make_async_copy(tab_rx, tab_s, local_sem.at[3])
    tab_copy.start()
    vote = tab_rx[0]
    for j in range(1, RING):
        vote = jnp.maximum(vote, tab_rx[j])
    vote_tx[...] = jnp.broadcast_to(vote[1:2], (8, TILE))
    vote_copies = [
        remote(vote_tx, vote_rx.at[j], vote_send.at[j], vote_recv.at[j], on_first(j)) for j in range(1, RING)
    ]
    for copy in vote_copies:
        start(copy)

    tab_copy.wait()

    def locate(s, carry):
        su, sv, st = source_of(s)
        distance = lax.rem(v - sv + RING, RING)
        for a in range(AB):
            slot = tab_s[distance, 0, su * MINE + st * AB + a]
            index_s[s * AB + a] = jnp.clip(slot, 0, ZERO_SLOT)
        return carry

    lax.fori_loop(0, NS, locate, 0)

    for hop in range(2, HOPS + 1):
        for piece in range(HOPS - hop + 1):
            for sign in range(2):
                second(sign, hop - 1, piece).wait_recv()
                start(second(sign, hop, piece))
    for copy in vote_copies:
        copy.wait_recv()
    vote = vote_tx[...]
    for j in range(1, RING):
        vote = jnp.maximum(vote, vote_rx[j])
    vote_wide = jnp.concatenate([vote, vote], axis=1).astype(jnp.float32)
    own_copy.wait()
    amp_copy.wait()
    for hop in range(1, HOPS + 1):
        for sign in range(2):
            second(sign, hop, HOPS - hop).wait_recv()

    total[...] = jnp.zeros_like(total)

    def multiply(i, carry):
        left = jnp.concatenate([amp[2 * i], amp[2 * i + 1]], axis=1)
        rows = [
            jnp.concatenate([pool[index_s[4 * i + 2 * h]], pool[index_s[4 * i + 2 * h + 1]]], axis=1)
            for h in range(2)
        ]
        total[...] += jnp.dot(left, jnp.concatenate(rows, axis=0), preferred_element_type=jnp.float32)
        return carry

    lax.fori_loop(0, NS // 2, multiply, 0)

    for q in range(KA):
        part_tx[q, 0:ROWS] = total[q * ROWS : (q + 1) * ROWS]
        part_tx[q, ROWS : ROWS + 8] = vote_wide
    part_copies = [
        remote(part_tx.at[lax.rem(ka + j, KA)], part_rx.at[j], part_send.at[j], part_recv.at[j], on_ka(j))
        for j in range(1, KA)
    ]
    for copy in part_copies:
        start(copy)
    result = part_tx[ka, 0:ROWS]
    for copy in part_copies:
        copy.wait_recv()
    vote = vote_wide
    for j in range(1, KA):
        result += part_rx[j, 0:ROWS]
        vote = jnp.maximum(vote, part_rx[j, ROWS : ROWS + 8])
    out_ref[...] = result
    flag_ref[...] = vote[:, 0:TILE]
    for copy in sent:
        copy.wait_send()


def ladder(amplitude, slot_owner, slot_tile, integrals, tile_mask):
    scratch = [
        pltpu.VMEM((NS, TILE, TILE), jnp.bfloat16),
        pltpu.VMEM((GROUP, TILE, TILE), jnp.bfloat16),
        pltpu.VMEM((2, CAPS[0], TILE, TILE), jnp.bfloat16),
        pltpu.VMEM((SLOTS, TILE, TILE), jnp.bfloat16),
        pltpu.VMEM((RING, 8, TILE), jnp.float32),
        pltpu.VMEM((RING, 8, TILE), jnp.float32),
        pltpu.VMEM((RING, 8, TILE), jnp.float32),
        pltpu.VMEM((2, 8, TILE), jnp.int32),
        pltpu.VMEM((RING, 8, TILE), jnp.int32),
        pltpu.VMEM((RING, 8, TILE), jnp.int32),
        pltpu.VMEM((8, TILE), jnp.int32),
        pltpu.VMEM((RING, 8, TILE), jnp.int32),
        pltpu.SMEM((2, 8, TILE), jnp.int32),
        pltpu.SMEM((RING, 8, TILE), jnp.int32),
        pltpu.SMEM((NS * AB,), jnp.int32),
        pltpu.VMEM((TILE, AB * TILE), jnp.float32),
        pltpu.VMEM((KA, ROWS + 8, AB * TILE), jnp.float32),
        pltpu.VMEM((KA, ROWS + 8, AB * TILE), jnp.float32),
        pltpu.SemaphoreType.DMA((4,)),
        pltpu.SemaphoreType.DMA((16,)),
        pltpu.SemaphoreType.DMA((16,)),
        pltpu.SemaphoreType.DMA((2 * HOPS * HOPS,)),
        pltpu.SemaphoreType.DMA((2 * HOPS * HOPS,)),
    ] + [pltpu.SemaphoreType.DMA((RING,)) for _ in range(10)]
    smem, vmem = pl.BlockSpec(memory_space=pltpu.SMEM), pl.BlockSpec(memory_space=pltpu.VMEM)
    return pl.pallas_call(
        kernel,
        out_shape=(
            jax.ShapeDtypeStruct((ROWS, AB * TILE), jnp.float32),
            jax.ShapeDtypeStruct((8, TILE), jnp.float32),
        ),
        in_specs=[smem, smem, smem, vmem, pl.BlockSpec(memory_space=pl.ANY)],
        out_specs=(vmem, vmem),
        scratch_shapes=scratch,
        compiler_params=pltpu.CompilerParams(
            collective_id=0, has_side_effects=True, vmem_limit_bytes=32 * 1024 * 1024
        ),
    )(slot_owner, slot_tile, tile_mask, integrals, amplitude)


def dense(amplitude, slot_owner, slot_tile, integrals, tile_mask):
    held, edge, columns = integrals.shape
    bands = columns // edge
    masked = (
        integrals.reshape(held, edge, bands, edge) * tile_mask.astype(jnp.bfloat16)[:, None, :, None]
    ).reshape(held, edge, columns)
    everything = lax.all_gather(masked, "pair", axis=0, tiled=True)
    chosen = jnp.take(everything, slot_owner * held + slot_tile, axis=0)
    rows = jnp.einsum("sij,sjk->ik", amplitude, chosen, preferred_element_type=jnp.float32)
    return lax.psum_scatter(rows, "ka", scatter_dimension=0, tiled=True)


def local(amplitude, slot_owner, slot_tile, integrals, tile_mask):
    result, flag = ladder(amplitude, slot_owner, slot_tile, integrals, tile_mask)
    return lax.cond(
        flag[0, 0] > 0.0,
        lambda: dense(amplitude, slot_owner, slot_tile, integrals, tile_mask),
        lambda: result,
    )


def solution(mesh):
    in_specs = (
        P(("pair", "ka"), None, None),
        P(("pair", "ka")),
        P(("pair", "ka")),
        P(("pair", "ka"), None, None),
        P(("pair", "ka"), None),
    )
    out_specs = P(("pair", "ka"), None)
    return jax.shard_map(local, mesh=mesh, in_specs=in_specs, out_specs=out_specs, check_vma=False)
```

time: 510 us -> 95.7 us (0.19)
  blocking collectives: 239 us -> 0 us
  waiting for transfers between devices: 214 us -> 0 us
  Pallas kernels: 0 us -> 78.7 us
  starting transfers between devices: 17.5 us -> 0 us
  other arithmetic: 12.3 us -> 0 us
  local copies, waits for them, and re-layouts: 8.51 us -> 2.6 us
    all_to_all x1 -> x0, blocking collectives: 239 us -> none  [local(): lax.all_to_all(partial_value, 'pair', split_axis=0, concat_axis=0, tiled=...]
    all_to_all x1 -> x0, waiting for transfers between devices: 168 us -> none  [local(): lax.all_to_all(panels, 'pair', split_axis=0, concat_axis=0, tiled=True)]
    pallas_call x0 -> x1, Pallas kernels: none -> 78.7 us  [ladder(): pl.pallas_call(kernel, out_shape=(jax.ShapeDtypeStruct((ROWS, AB * TILE),...]
    reduce_scatter x1 -> x0, waiting for transfers between devices: 45.3 us -> none  [local(): return lax.psum_scatter(residual, 'ka', scatter_dimension=0, tiled=True)]
    all_to_all x1 -> x0, starting transfers between devices: 17.5 us -> none  [local(): lax.all_to_all(panels, 'pair', split_axis=0, concat_axis=0, tiled=True)]
    gather x1 -> x0, local copies, waits for them, and re-layouts: 7.92 us -> none  [local(): picked = jnp.take(amplitude, chosen, axis=0)]
    select_n x2 -> x0, other arithmetic: 6.74 us -> none  [the longest x1 6.73 us: local(): jnp.where(present[:, None, None], picked, jnp.zeros((), jnp.bfloat16))]
  transfers between devices with their start and end apart: 2 -> 0, of which waited for: 2 -> 0; matrix products, arithmetic and copies ran while one was open for 0% -> 0% of each run, Pallas kernels for 0% -> 0%
where the time goes in v1:
time: 95.7 us; the launch traced here: 95.3 us
  Pallas kernels  78.7 us (82%)
  between operations  14 us (15%)
  local copies, waits for them, and re-layouts  2.6 us (3%)
    pallas_call x1, Pallas kernels, ladder(): pl.pallas_call(kernel, out_shape=(jax.ShapeDtypeStruct((ROWS, AB * TILE),...  78.7 us
    unnamed x2, local copies, waits for them, and re-layouts  2.09 us

profile of v1, /device:TPU:1, one launch (start us, length us, event | category | flops | bytes accessed | tf_op | source)
XLA Modules:
  0.0 95.3 jit_solution(9819669189783902921)
XLA Ops:
  6.5 0.8 copy.14.mask_ref
  7.3 78.7 %shard_map.57 = (f32[16,256]{1,0:T(8,128)}, f32[8,128]{1,0:T(8,128)S(1)}) custom-call(s32[48]{0:T(128)} %owner_ref.1, s32[48]{0:T(128)} %tile_ref.1, s32[3,2]{1,0:T(4,128)S(1)} %copy.14.mask_ref, bf16[3,128,256]{2,1,0:T(8,128)(2,1)} %integrals_ref.1, bf16[48,128,128]{2,1,0:T(8,128)(2,1)} %amplitude_ref.1), custom_call_target="tpu_custom_call" | custom-call | tf_op jit(solution)/shard_map/pallas_call | solution.py:326
  86.0 0.5 slice.3
  87.1 1.3 %copy.29 = f32[16,256]{1,0:T(8,128)} copy(f32[16,256]{1,0:T(8,128)} %get-tuple-element.34) | data formatting | bytes 32768
  (1 shorter events, 0.0 us)

commit v2 on v1

--- a/solution.py
+++ b/solution.py
@@ -18,11 +18,25 @@
 MINE = HELD * AB
 GROUP = RING * MINE
 HALF = MINE // 2
+STEP = 8
 ROWS = TILE // KA
 
-CAPS = (30, 28, 24, 12)
+CAPS = (30, 29, 25, 12)
 HOPS = len(CAPS)
-CUTS = (0,) + CAPS[::-1]
+LONGEST = 8
+
+
+def cut_lists():
+    pieces = []
+    for hops, (begin, end) in zip(range(HOPS, 0, -1), zip((0,) + CAPS[::-1], CAPS[::-1])):
+        count = -(-(end - begin) // LONGEST)
+        for i in range(count):
+            left, right = (end - begin) * i // count, (end - begin) * (i + 1) // count
+            pieces.append((begin + left, right - left, hops))
+    return pieces
+
+
+PIECES = cut_lists()
 
 
 def region(sign, hop):
@@ -57,6 +71,17 @@
     def on_ka(step):
         return (pair, lax.rem(ka + step, KA))
 
+    load_copies = [
+        pltpu.make_async_copy(
+            integrals_ref.at[:, :, pl.ds(a * TILE, TILE)],
+            group.at[pl.ds(u * MINE + a * HELD, HELD)],
+            local_sem.at[4 + a],
+        )
+        for a in range(AB)
+    ]
+    for copy in load_copies:
+        copy.start()
+
     barrier = pltpu.get_barrier_semaphore()
     for step in range(1, RING):
         for there in (on_first(step), on_second(step), on_ka(step)):
@@ -65,38 +90,36 @@
     amp_copy = pltpu.make_async_copy(amplitude_ref, amp, local_sem.at[0])
     amp_copy.start()
 
-    for t in range(HELD):
-        for a in range(AB):
-            block = integrals_ref[t, :, a * TILE : (a + 1) * TILE].astype(jnp.float32)
-            scale = mask_ref[t, a].astype(jnp.float32)
-            group[u * MINE + t * AB + a] = (block * scale).astype(jnp.bfloat16)
-
     lane = lax.broadcasted_iota(jnp.int32, (8, TILE), 1)
     own_mask = jnp.zeros((8, TILE), jnp.float32)
     for t in range(HELD):
         for a in range(AB):
-            here = lane == u * MINE + t * AB + a
-            own_mask = jnp.where(here, mask_ref[t, a].astype(jnp.float32), own_mask)
+            here = lane == u * MINE + a * HELD + t
+            own_mask = jnp.where(here, mask_ref[t : t + 1, a : a + 1].astype(jnp.float32), own_mask)
     mask_rx[0] = own_mask
 
     def source_of(s):
         owner = owner_ref[s]
-        oh, ol = owner // RING, lax.rem(owner, RING)
+        oh, ol = lax.div(owner, RING), lax.rem(owner, RING)
         return oh + core * (ol - oh), ol + core * (oh - ol), tile_ref[s]
 
     code = lax.broadcasted_iota(jnp.int32, (RING, 8, TILE), 0) * TILE + lax.broadcasted_iota(
         jnp.int32, (RING, 8, TILE), 2
-    ) // AB
+    )
 
     def mark(s, seen):
         su, sv, st = source_of(s)
         distance = lax.rem(sv - v + RING, RING)
-        return jnp.where(code == distance * TILE + su * HELD + st, 1.0, seen)
+        for a in range(AB):
+            seen = jnp.where(code == distance * TILE + su * MINE + a * HELD + st, 1.0, seen)
+        return seen
 
     need_tx[...] = lax.fori_loop(0, NS, mark, jnp.zeros((RING, 8, TILE), jnp.float32))
 
     pool[ZERO_SLOT] = jnp.zeros((TILE, TILE), jnp.bfloat16)
 
+    for copy in load_copies:
+        copy.wait()
     pl.semaphore_wait(barrier, 3 * (RING - 1))
 
     def remote(src, dst, send, recv, there):
@@ -134,11 +157,13 @@
         start(copy)
     for sign in range(2):
         start(first(sign, 1, 1))
-    for hop in (2, 3):
+    def forward(hop):
         for chunk in range(2):
             for sign in range(2):
                 first_arrival(sign, hop - 1, chunk).wait_recv()
                 start(first(sign, hop, chunk))
+
+    forward(2)
 
     for copy in need_copies + mask_copies:
         copy.wait_recv()
@@ -149,19 +174,23 @@
     flane = lane.astype(jnp.float32)
     wide_lane = lax.broadcasted_iota(jnp.int32, (GROUP, TILE), 1)
     wide_row = lax.broadcasted_iota(jnp.int32, (GROUP, TILE), 0)
+    far = []
+    for sign in range(2):
+        reach = jnp.zeros((8, TILE), jnp.float32)
+        for distance in range(1, HOPS):
+            needed = need_rx[distance if sign else RING - distance] * mask
+            reach = jnp.where(needed > 0.0, float(distance), reach)
+        far.append(reach)
+    opposite = need_rx[HOPS] * mask > 0.0
+    far[0] = jnp.where(jnp.logical_and(opposite, even), float(HOPS), far[0])
+    far[1] = jnp.where(jnp.logical_and(opposite, jnp.logical_not(even)), float(HOPS), far[1])
     ranks = []
     over = jnp.zeros((8, TILE), jnp.float32)
     for sign in range(2):
-        far = jnp.zeros((8, TILE), jnp.float32)
-        for distance in range(1, HOPS + 1):
-            needed = need_rx[distance if sign else RING - distance] * mask
-            if distance == HOPS:
-                needed = jnp.where(even == (sign == 0), needed, 0.0)
-            far = jnp.where(needed > 0.0, float(distance), far)
         for hop in range(1, HOPS + 1):
-            count = jnp.sum(jnp.where(far >= float(hop), 1.0, 0.0), axis=1, keepdims=True)
+            count = jnp.sum(jnp.where(far[sign] >= float(hop), 1.0, 0.0), axis=1, keepdims=True)
             over = jnp.maximum(over, jnp.where(count > float(CAPS[hop - 1]), 1.0, 0.0))
-        key = far * float(TILE) + (float(TILE - 1) - flane)
+        key = far[sign] * float(TILE) + (float(TILE - 1) - flane)
         key_row = jnp.broadcast_to(key[0:1], (GROUP, TILE))
         key_col = jnp.sum(jnp.where(wide_lane == wide_row, key_row, 0.0), axis=1, keepdims=True)
         rank_row = jnp.sum(jnp.where(key_col > key_row, 1.0, 0.0), axis=0, keepdims=True)
@@ -172,6 +201,7 @@
         ranks.append(jnp.broadcast_to(rank_row, (8, TILE)))
     order_copy = pltpu.make_async_copy(order, order_s, local_sem.at[1])
     order_copy.start()
+    forward(3)
 
     sub = lax.broadcasted_iota(jnp.int32, (8, TILE), 0)
     for j in range(1, RING):
@@ -183,38 +213,34 @@
     tab_copies = [
         remote(tab_tx.at[j], tab_rx.at[j], tab_send.at[j], tab_recv.at[j], on_second(j)) for j in range(1, RING)
     ]
-    tab_rx[0] = jnp.where(sub == 0, lane, over.astype(jnp.int32))
+    tab_rx[0] = jnp.where(sub == 0, jnp.where(mask > 0.0, flane, float(ZERO_SLOT)), over).astype(jnp.int32)
 
     for sign in range(2):
         first_arrival(sign, 3, sign).wait_recv()
         start(first(sign, 4, sign))
+    order_copy.wait()
     for sign in range(2):
         first_arrival(sign, 3, 1 - sign).wait_recv()
-    for copy in tab_copies:
-        start(copy)
-    order_copy.wait()
     for sign in range(2):
         first_arrival(sign, 4, sign).wait_recv()
 
     def second(sign, hop, piece):
-        begin, size = CUTS[piece], CUTS[piece + 1] - CUTS[piece]
+        begin, size, _ = PIECES[piece]
         if hop == 1:
             src = lists.at[sign, pl.ds(begin, size)]
         else:
             src = pool.at[pl.ds(region(sign, hop - 1) + begin, size)]
         dst = pool.at[pl.ds(region(sign, hop) + begin, size)]
-        number = (sign * HOPS + hop - 1) * HOPS + piece
+        number = (sign * HOPS + hop - 1) * len(PIECES) + piece
         return remote(src, dst, two_send.at[number], two_recv.at[number], on_second(-1 if sign else 1))
 
-    for piece in range(HOPS):
+    for piece, (begin, size, _) in enumerate(PIECES):
         for sign in range(2):
-
-            def pick(r, carry, sign=sign):
+            for r in range(begin, begin + size):
                 lists[sign, r] = group[jnp.clip(order_s[sign, 0, r], 0, GROUP - 1)]
-                return carry
-
-            lax.fori_loop(CUTS[piece], CUTS[piece + 1], pick, 0)
             start(second(sign, 1, piece))
+    for copy in tab_copies:
+        start(copy)
     own_copy = pltpu.make_async_copy(group, pool.at[pl.ds(0, GROUP)], local_sem.at[2])
     own_copy.start()
 
@@ -238,17 +264,18 @@
         su, sv, st = source_of(s)
         distance = lax.rem(v - sv + RING, RING)
         for a in range(AB):
-            slot = tab_s[distance, 0, su * MINE + st * AB + a]
+            slot = tab_s[distance, 0, su * MINE + a * HELD + st]
             index_s[s * AB + a] = jnp.clip(slot, 0, ZERO_SLOT)
         return carry
 
     lax.fori_loop(0, NS, locate, 0)
 
     for hop in range(2, HOPS + 1):
-        for piece in range(HOPS - hop + 1):
-            for sign in range(2):
-                second(sign, hop - 1, piece).wait_recv()
-                start(second(sign, hop, piece))
+        for piece, (_, _, hops) in enumerate(PIECES):
+            if hops >= hop:
+                for sign in range(2):
+                    second(sign, hop - 1, piece).wait_recv()
+                    start(second(sign, hop, piece))
     for copy in vote_copies:
         copy.wait_recv()
     vote = vote_tx[...]
@@ -257,22 +284,23 @@
     vote_wide = jnp.concatenate([vote, vote], axis=1).astype(jnp.float32)
     own_copy.wait()
     amp_copy.wait()
-    for hop in range(1, HOPS + 1):
+    for piece, (_, _, hops) in enumerate(PIECES):
         for sign in range(2):
-            second(sign, hop, HOPS - hop).wait_recv()
+            second(sign, hops, piece).wait_recv()
 
     total[...] = jnp.zeros_like(total)
 
     def multiply(i, carry):
-        left = jnp.concatenate([amp[2 * i], amp[2 * i + 1]], axis=1)
-        rows = [
-            jnp.concatenate([pool[index_s[4 * i + 2 * h]], pool[index_s[4 * i + 2 * h + 1]]], axis=1)
-            for h in range(2)
+        tiles = [amp[STEP * i + j] for j in range(STEP)]
+        bands = [
+            jnp.concatenate([pool[index_s[(STEP * i + j) * AB + a]] for j in range(STEP)], axis=0) for a in range(AB)
         ]
-        total[...] += jnp.dot(left, jnp.concatenate(rows, axis=0), preferred_element_type=jnp.float32)
+        total[...] += jnp.dot(
+            jnp.concatenate(tiles, axis=1), jnp.concatenate(bands, axis=1), preferred_element_type=jnp.float32
+        )
         return carry
 
-    lax.fori_loop(0, NS // 2, multiply, 0)
+    lax.fori_loop(0, NS // STEP, multiply, 0)
 
     for q in range(KA):
         part_tx[q, 0:ROWS] = total[q * ROWS : (q + 1) * ROWS]
@@ -282,7 +310,9 @@
         for j in range(1, KA)
     ]
     for copy in part_copies:
-        start(copy)
+        copy.start()
+    for copy in sent:
+        copy.wait_send()
     result = part_tx[ka, 0:ROWS]
     for copy in part_copies:
         copy.wait_recv()
@@ -292,7 +322,7 @@
         vote = jnp.maximum(vote, part_rx[j, ROWS : ROWS + 8])
     out_ref[...] = result
     flag_ref[...] = vote[:, 0:TILE]
-    for copy in sent:
+    for copy in part_copies:
         copy.wait_send()
 
 
@@ -316,20 +346,21 @@
         pltpu.VMEM((TILE, AB * TILE), jnp.float32),
         pltpu.VMEM((KA, ROWS + 8, AB * TILE), jnp.float32),
         pltpu.VMEM((KA, ROWS + 8, AB * TILE), jnp.float32),
-        pltpu.SemaphoreType.DMA((4,)),
+        pltpu.SemaphoreType.DMA((6,)),
         pltpu.SemaphoreType.DMA((16,)),
         pltpu.SemaphoreType.DMA((16,)),
-        pltpu.SemaphoreType.DMA((2 * HOPS * HOPS,)),
-        pltpu.SemaphoreType.DMA((2 * HOPS * HOPS,)),
+        pltpu.SemaphoreType.DMA((2 * HOPS * len(PIECES),)),
+        pltpu.SemaphoreType.DMA((2 * HOPS * len(PIECES),)),
     ] + [pltpu.SemaphoreType.DMA((RING,)) for _ in range(10)]
     smem, vmem = pl.BlockSpec(memory_space=pltpu.SMEM), pl.BlockSpec(memory_space=pltpu.VMEM)
+    hbm = pl.BlockSpec(memory_space=pl.ANY)
     return pl.pallas_call(
         kernel,
         out_shape=(
             jax.ShapeDtypeStruct((ROWS, AB * TILE), jnp.float32),
             jax.ShapeDtypeStruct((8, TILE), jnp.float32),
         ),
-        in_specs=[smem, smem, smem, vmem, pl.BlockSpec(memory_space=pl.ANY)],
+        in_specs=[smem, smem, vmem, hbm, hbm],
         out_specs=(vmem, vmem),
         scratch_shapes=scratch,
         compiler_params=pltpu.CompilerParams(

time: 95.7 us -> 101 us (1.055)
  Pallas kernels: 78.7 us -> 84.6 us
    pallas_call x1, Pallas kernels: 78.7 us -> 84.6 us  [ladder(): pl.pallas_call(kernel, out_shape=(jax.ShapeDtypeStruct((ROWS, AB * TILE),...]
where the time goes in v2:
time: 101 us
  Pallas kernels  84.6 us (84%)
  between operations  14 us (14%)
  local copies, waits for them, and re-layouts  2.6 us (3%)
    pallas_call x1, Pallas kernels, ladder(): pl.pallas_call(kernel, out_shape=(jax.ShapeDtypeStruct((ROWS, AB * TILE),...  84.6 us
    unnamed x2, local copies, waits for them, and re-layouts  2.09 us

profile of v2, /device:TPU:1, one launch (start us, length us, event | category | flops | bytes accessed | tf_op | source)
XLA Modules:
  0.0 101.2 jit_solution(10029868360257605955)
XLA Ops:
  6.5 0.8 copy.14.mask_ref
  7.3 84.6 %shard_map.57 = (f32[16,256]{1,0:T(8,128)}, f32[8,128]{1,0:T(8,128)S(1)}) custom-call(s32[48]{0:T(128)} %owner_ref.1, s32[48]{0:T(128)} %tile_ref.1, s32[3,2]{1,0:T(4,128)S(1)} %copy.14.mask_ref, bf16[3,128,256]{2,1,0:T(8,128)(2,1)} %integrals_ref.1, bf16[48,128,128]{2,1,0:T(8,128)(2,1)} %amplitude_ref.1), custom_call_target="tpu_custom_call" | custom-call | tf_op jit(solution)/shard_map/pallas_call | solution.py:357
  91.9 0.5 slice.3
  93.0 1.3 %copy.29 = f32[16,256]{1,0:T(8,128)} copy(f32[16,256]{1,0:T(8,128)} %get-tuple-element.34) | data formatting | bytes 32768
  (1 shorter events, 0.0 us)

commit v3 on v2

--- a/solution.py
+++ b/solution.py
@@ -17,38 +17,34 @@
 KA = 8
 MINE = HELD * AB
 GROUP = RING * MINE
-HALF = MINE // 2
 STEP = 8
 ROWS = TILE // KA
 
-CAPS = (30, 29, 25, 12)
-HOPS = len(CAPS)
+HOPS = RING // 2
 LONGEST = 8
 
-
-def cut_lists():
-    pieces = []
-    for hops, (begin, end) in zip(range(HOPS, 0, -1), zip((0,) + CAPS[::-1], CAPS[::-1])):
-        count = -(-(end - begin) // LONGEST)
-        for i in range(count):
-            left, right = (end - begin) * i // count, (end - begin) * (i + 1) // count
-            pieces.append((begin + left, right - left, hops))
-    return pieces
-
-
-PIECES = cut_lists()
-
-
-def region(sign, hop):
-    return GROUP + sign * sum(CAPS) + sum(CAPS[: hop - 1])
-
-
-ZERO_SLOT = GROUP + 2 * sum(CAPS)
-SLOTS = ZERO_SLOT + 1
+USUAL = (30, 28, 25, 12)
+EVERY = (GROUP, GROUP, GROUP, GROUP // 2)
+
+
+class Plan:
+    def __init__(self, caps):
+        self.caps = caps
+        self.zero_slot = GROUP + 2 * sum(caps)
+        self.slots = self.zero_slot + 1
+        self.pieces = []
+        for hops, begin, end in zip(range(HOPS, 0, -1), (0,) + caps[::-1], caps[::-1]):
+            count = -(-(end - begin) // LONGEST)
+            for i in range(count):
+                left, right = (end - begin) * i // count, (end - begin) * (i + 1) // count
+                self.pieces.append((begin + left, right - left, hops))
+
+    def region(self, sign, hop):
+        return GROUP + sign * sum(self.caps) + sum(self.caps[: hop - 1])
 
 
 def kernel(
-    owner_ref, tile_ref, mask_ref, integrals_ref, amplitude_ref,
+    plan, owner_ref, tile_ref, mask_ref, integrals_ref, amplitude_ref,
     out_ref, flag_ref,
     amp, group, lists, pool, need_tx, need_rx, mask_rx, order, tab_tx, tab_rx, vote_tx, vote_rx,
     order_s, tab_s, index_s, total, part_tx, part_rx,
@@ -95,7 +91,7 @@
     for t in range(HELD):
         for a in range(AB):
             here = lane == u * MINE + a * HELD + t
-            own_mask = jnp.where(here, mask_ref[t : t + 1, a : a + 1].astype(jnp.float32), own_mask)
+            own_mask = jnp.where(here, mask_ref[a : a + 1, t : t + 1].astype(jnp.float32), own_mask)
     mask_rx[0] = own_mask
 
     def source_of(s):
@@ -116,7 +112,7 @@
 
     need_tx[...] = lax.fori_loop(0, NS, mark, jnp.zeros((RING, 8, TILE), jnp.float32))
 
-    pool[ZERO_SLOT] = jnp.zeros((TILE, TILE), jnp.bfloat16)
+    pool[plan.zero_slot] = jnp.zeros((TILE, TILE), jnp.bfloat16)
 
     for copy in load_copies:
         copy.wait()
@@ -127,17 +123,14 @@
             src_ref=src, dst_ref=dst, send_sem=send, recv_sem=recv, device_id=there, device_id_type=MESH
         )
 
-    def first(sign, hop, chunk):
-        behind = lax.rem(u + (hop - 1 if sign else RING - hop + 1), RING)
-        ref = group.at[pl.ds(behind * MINE + chunk * HALF, HALF)]
-        number = (sign * 4 + hop - 1) * 2 + chunk
+    def first(sign, hop, block, arrival=False):
+        behind = lax.rem(u + (hop - 1 + arrival if sign else RING - hop + 1 - arrival), RING)
+        ref = group.at[pl.ds(behind * MINE + block, 1)]
+        number = (sign * HOPS + hop - 1) * MINE + block
         return remote(ref, ref, one_send.at[number], one_recv.at[number], on_first(-1 if sign else 1))
 
-    def first_arrival(sign, hop, chunk):
-        behind = lax.rem(u + (hop if sign else RING - hop), RING)
-        ref = group.at[pl.ds(behind * MINE + chunk * HALF, HALF)]
-        number = (sign * 4 + hop - 1) * 2 + chunk
-        return remote(ref, ref, one_send.at[number], one_recv.at[number], on_first(-1 if sign else 1))
+    def first_wait(sign, hop, block):
+        first(sign, hop, block, arrival=True).wait_recv()
 
     need_copies = [
         remote(need_tx.at[j], need_rx.at[j], need_send.at[j], need_recv.at[j], on_second(j)) for j in range(1, RING)
@@ -151,17 +144,18 @@
         copy.start()
         sent.append(copy)
 
-    for sign in range(2):
-        start(first(sign, 1, 0))
-    for copy in need_copies + mask_copies:
-        start(copy)
-    for sign in range(2):
-        start(first(sign, 1, 1))
+    for block in range(MINE):
+        for sign in range(2):
+            start(first(sign, 1, block))
+        if block == 1:
+            for copy in need_copies + mask_copies:
+                start(copy)
+
     def forward(hop):
-        for chunk in range(2):
+        for block in range(MINE):
             for sign in range(2):
-                first_arrival(sign, hop - 1, chunk).wait_recv()
-                start(first(sign, hop, chunk))
+                first_wait(sign, hop - 1, block)
+                start(first(sign, hop, block))
 
     forward(2)
 
@@ -189,7 +183,7 @@
     for sign in range(2):
         for hop in range(1, HOPS + 1):
             count = jnp.sum(jnp.where(far[sign] >= float(hop), 1.0, 0.0), axis=1, keepdims=True)
-            over = jnp.maximum(over, jnp.where(count > float(CAPS[hop - 1]), 1.0, 0.0))
+            over = jnp.maximum(over, jnp.where(count > float(plan.caps[hop - 1]), 1.0, 0.0))
         key = far[sign] * float(TILE) + (float(TILE - 1) - flane)
         key_row = jnp.broadcast_to(key[0:1], (GROUP, TILE))
         key_col = jnp.sum(jnp.where(wide_lane == wide_row, key_row, 0.0), axis=1, keepdims=True)
@@ -205,42 +199,43 @@
 
     sub = lax.broadcasted_iota(jnp.int32, (8, TILE), 0)
     for j in range(1, RING):
-        right = ranks[0] + float(region(0, min(j, HOPS)))
-        left = ranks[1] + float(region(1, min(RING - j, HOPS)))
+        right = ranks[0] + float(plan.region(0, min(j, HOPS)))
+        left = ranks[1] + float(plan.region(1, min(RING - j, HOPS)))
         slot = right if j < HOPS else left if j > HOPS else jnp.where(even, right, left)
-        slot = jnp.where(mask > 0.0, slot, float(ZERO_SLOT))
+        slot = jnp.where(mask > 0.0, slot, float(plan.zero_slot))
         tab_tx[j] = jnp.where(sub == 0, slot, over).astype(jnp.int32)
     tab_copies = [
         remote(tab_tx.at[j], tab_rx.at[j], tab_send.at[j], tab_recv.at[j], on_second(j)) for j in range(1, RING)
     ]
-    tab_rx[0] = jnp.where(sub == 0, jnp.where(mask > 0.0, flane, float(ZERO_SLOT)), over).astype(jnp.int32)
-
-    for sign in range(2):
-        first_arrival(sign, 3, sign).wait_recv()
-        start(first(sign, 4, sign))
+    tab_rx[0] = jnp.where(sub == 0, jnp.where(mask > 0.0, flane, float(plan.zero_slot)), over).astype(jnp.int32)
+
+    for copy in tab_copies:
+        start(copy)
+
+    for block in range(MINE):
+        for sign in range(2):
+            first_wait(sign, HOPS - 1, block)
+            if block % 2 == sign:
+                start(first(sign, HOPS, block))
     order_copy.wait()
-    for sign in range(2):
-        first_arrival(sign, 3, 1 - sign).wait_recv()
-    for sign in range(2):
-        first_arrival(sign, 4, sign).wait_recv()
+    for block in range(MINE):
+        first_wait(block % 2, HOPS, block)
 
     def second(sign, hop, piece):
-        begin, size, _ = PIECES[piece]
+        begin, size, _ = plan.pieces[piece]
         if hop == 1:
             src = lists.at[sign, pl.ds(begin, size)]
         else:
-            src = pool.at[pl.ds(region(sign, hop - 1) + begin, size)]
-        dst = pool.at[pl.ds(region(sign, hop) + begin, size)]
-        number = (sign * HOPS + hop - 1) * len(PIECES) + piece
+            src = pool.at[pl.ds(plan.region(sign, hop - 1) + begin, size)]
+        dst = pool.at[pl.ds(plan.region(sign, hop) + begin, size)]
+        number = (sign * HOPS + hop - 1) * len(plan.pieces) + piece
         return remote(src, dst, two_send.at[number], two_recv.at[number], on_second(-1 if sign else 1))
 
-    for piece, (begin, size, _) in enumerate(PIECES):
+    for piece, (begin, size, _) in enumerate(plan.pieces):
         for sign in range(2):
             for r in range(begin, begin + size):
                 lists[sign, r] = group[jnp.clip(order_s[sign, 0, r], 0, GROUP - 1)]
             start(second(sign, 1, piece))
-    for copy in tab_copies:
-        start(copy)
     own_copy = pltpu.make_async_copy(group, pool.at[pl.ds(0, GROUP)], local_sem.at[2])
     own_copy.start()
 
@@ -265,13 +260,13 @@
         distance = lax.rem(v - sv + RING, RING)
         for a in range(AB):
             slot = tab_s[distance, 0, su * MINE + a * HELD + st]
-            index_s[s * AB + a] = jnp.clip(slot, 0, ZERO_SLOT)
+            index_s[s * AB + a] = jnp.clip(slot, 0, plan.zero_slot)
         return carry
 
     lax.fori_loop(0, NS, locate, 0)
 
     for hop in range(2, HOPS + 1):
-        for piece, (_, _, hops) in enumerate(PIECES):
+        for piece, (_, _, hops) in enumerate(plan.pieces):
             if hops >= hop:
                 for sign in range(2):
                     second(sign, hop - 1, piece).wait_recv()
@@ -284,7 +279,7 @@
     vote_wide = jnp.concatenate([vote, vote], axis=1).astype(jnp.float32)
     own_copy.wait()
     amp_copy.wait()
-    for piece, (_, _, hops) in enumerate(PIECES):
+    for piece, (_, _, hops) in enumerate(plan.pieces):
         for sign in range(2):
             second(sign, hops, piece).wait_recv()
 
@@ -321,17 +316,17 @@
         result += part_rx[j, 0:ROWS]
         vote = jnp.maximum(vote, part_rx[j, ROWS : ROWS + 8])
     out_ref[...] = result
-    flag_ref[...] = vote[:, 0:TILE]
+    flag_ref[0] = jnp.max(vote).astype(jnp.int32)
     for copy in part_copies:
         copy.wait_send()
 
 
-def ladder(amplitude, slot_owner, slot_tile, integrals, tile_mask):
+def ladder(plan, number, amplitude, slot_owner, slot_tile, integrals, tile_mask):
     scratch = [
         pltpu.VMEM((NS, TILE, TILE), jnp.bfloat16),
         pltpu.VMEM((GROUP, TILE, TILE), jnp.bfloat16),
-        pltpu.VMEM((2, CAPS[0], TILE, TILE), jnp.bfloat16),
-        pltpu.VMEM((SLOTS, TILE, TILE), jnp.bfloat16),
+        pltpu.VMEM((2, plan.caps[0], TILE, TILE), jnp.bfloat16),
+        pltpu.VMEM((plan.slots, TILE, TILE), jnp.bfloat16),
         pltpu.VMEM((RING, 8, TILE), jnp.float32),
         pltpu.VMEM((RING, 8, TILE), jnp.float32),
         pltpu.VMEM((RING, 8, TILE), jnp.float32),
@@ -347,47 +342,31 @@
         pltpu.VMEM((KA, ROWS + 8, AB * TILE), jnp.float32),
         pltpu.VMEM((KA, ROWS + 8, AB * TILE), jnp.float32),
         pltpu.SemaphoreType.DMA((6,)),
-        pltpu.SemaphoreType.DMA((16,)),
-        pltpu.SemaphoreType.DMA((16,)),
-        pltpu.SemaphoreType.DMA((2 * HOPS * len(PIECES),)),
-        pltpu.SemaphoreType.DMA((2 * HOPS * len(PIECES),)),
+        pltpu.SemaphoreType.DMA((2 * HOPS * MINE,)),
+        pltpu.SemaphoreType.DMA((2 * HOPS * MINE,)),
+        pltpu.SemaphoreType.DMA((2 * HOPS * len(plan.pieces),)),
+        pltpu.SemaphoreType.DMA((2 * HOPS * len(plan.pieces),)),
     ] + [pltpu.SemaphoreType.DMA((RING,)) for _ in range(10)]
     smem, vmem = pl.BlockSpec(memory_space=pltpu.SMEM), pl.BlockSpec(memory_space=pltpu.VMEM)
     hbm = pl.BlockSpec(memory_space=pl.ANY)
     return pl.pallas_call(
-        kernel,
+        functools.partial(kernel, plan),
         out_shape=(
             jax.ShapeDtypeStruct((ROWS, AB * TILE), jnp.float32),
-            jax.ShapeDtypeStruct((8, TILE), jnp.float32),
+            jax.ShapeDtypeStruct((1,), jnp.int32),
         ),
         in_specs=[smem, smem, vmem, hbm, hbm],
-        out_specs=(vmem, vmem),
+        out_specs=(vmem, smem),
         scratch_shapes=scratch,
         compiler_params=pltpu.CompilerParams(
-            collective_id=0, has_side_effects=True, vmem_limit_bytes=32 * 1024 * 1024
+            collective_id=number, has_side_effects=True, vmem_limit_bytes=32 * 1024 * 1024
         ),
-    )(slot_owner, slot_tile, tile_mask, integrals, amplitude)
-
-
-def dense(amplitude, slot_owner, slot_tile, integrals, tile_mask):
-    held, edge, columns = integrals.shape
-    bands = columns // edge
-    masked = (
-        integrals.reshape(held, edge, bands, edge) * tile_mask.astype(jnp.bfloat16)[:, None, :, None]
-    ).reshape(held, edge, columns)
-    everything = lax.all_gather(masked, "pair", axis=0, tiled=True)
-    chosen = jnp.take(everything, slot_owner * held + slot_tile, axis=0)
-    rows = jnp.einsum("sij,sjk->ik", amplitude, chosen, preferred_element_type=jnp.float32)
-    return lax.psum_scatter(rows, "ka", scatter_dimension=0, tiled=True)
-
-
-def local(amplitude, slot_owner, slot_tile, integrals, tile_mask):
-    result, flag = ladder(amplitude, slot_owner, slot_tile, integrals, tile_mask)
-    return lax.cond(
-        flag[0, 0] > 0.0,
-        lambda: dense(amplitude, slot_owner, slot_tile, integrals, tile_mask),
-        lambda: result,
-    )
+    )(slot_owner, slot_tile, tile_mask.T, integrals, amplitude)
+
+
+def local(*arrays):
+    result, over = ladder(Plan(USUAL), 0, *arrays)
+    return lax.cond(over[0] > 0, lambda: ladder(Plan(EVERY), 1, *arrays)[0], lambda: result)
 
 
 def solution(mesh):

time: 101 us -> 77.5 us (0.77)
  between operations: 14 us -> 0.76 us
  Pallas kernels: 84.6 us -> 76 us
  local copies, waits for them, and re-layouts: 2.6 us -> 0.63 us
    pallas_call x1, Pallas kernels: 84.6 us -> 76 us  [ladder(): pl.pallas_call(functools.partial(kernel, plan), out_shape=(jax.ShapeDtype...]
    unnamed x2 -> x11, local copies, waits for them, and re-layouts: 2.09 us -> 0.63 us
where the time goes in v3:
time: 77.5 us; the launch traced here: 77.4 us
  Pallas kernels  76 us (98%)
    pallas_call x1, Pallas kernels, ladder(): pl.pallas_call(functools.partial(kernel, plan), out_shape=(jax.ShapeDtype...  76 us

profile of v3, /device:TPU:1, one launch (start us, length us, event | category | flops | bytes accessed | tf_op | source)
XLA Modules:
  0.0 77.4 jit_solution(3539632685937314930)
XLA Ops:
  0.0 0.0 copy-start.2
  0.0 0.0 copy-start.1
  0.0 0.0 copy-start.4
  0.0 0.0 copy-start.3
  0.0 0.0 copy-start
  0.0 76.0 %shard_map.57 = (f32[16,256]{1,0:T(8,128)S(1)}, s32[1]{0:T(128)}) custom-call(s32[48]{0:T(128)} %owner_ref.1, s32[48]{0:T(128)} %tile_ref.1, s32[2,3]{1,0:T(2,128)} %bitcast.3, bf16[3,128,256]{2,1,0:T(8,128)(2,1)} %integrals_ref.1, bf16[48,128,128]{2,1,0:T(8,128)(2,1)} %amplitude_ref.1), custom_call_target="tpu_custom_call" | custom-call | tf_op jit(solution)/shard_map/pallas_call | solution.py:352
  76.7 0.0 copy-done.2
  76.7 0.0 copy-done.1
  76.7 0.0 copy-done.4
  76.7 0.0 copy-done.3
  76.7 0.0 copy-done
  76.8 0.6 copy.11
  (1 shorter events, 0.0 us)
Async XLA Ops:
  0.0 76.7 %copy-start.2 = (s32[3,2]{0,1:T(2,128)S(1)}, s32[3,2]{0,1:T(2,128)}, u32[]{:S(2)}) copy-start(s32[3,2]{0,1:T(2,128)} %param.11) | copy-start | bytes 76
  0.0 76.7 %copy-start.1 = (bf16[3,128,256]{2,1,0:T(8,128)(2,1)S(1)}, bf16[3,128,256]{2,1,0:T(8,128)(2,1)}, u32[]{:S(2)}) copy-start(bf16[3,128,256]{2,1,0:T(8,128)(2,1)} %integrals_ref.1) | copy-start | bytes 589828
  0.0 76.7 %copy-start.4 = (s32[48]{0:T(128)S(1)}, s32[48]{0:T(128)}, u32[]{:S(2)}) copy-start(s32[48]{0:T(128)} %tile_ref.1) | copy-start | bytes 580
  0.0 76.7 %copy-start.3 = (s32[48]{0:T(128)S(1)}, s32[48]{0:T(128)}, u32[]{:S(2)}) copy-start(s32[48]{0:T(128)} %owner_ref.1) | copy-start | bytes 580
  0.0 76.7 %copy-start = (bf16[48,128,128]{2,1,0:T(8,128)(2,1)S(1)}, bf16[48,128,128]{2,1,0:T(8,128)(2,1)}, u32[]{:S(2)}) copy-start(bf16[48,128,128]{2,1,0:T(8,128)(2,1)} %amplitude_ref.1) | copy-start | bytes 4718596

commit v4 on v3

v4 whole, which is shorter than its diff:
```python
import functools

import jax
import jax.numpy as jnp
from jax import lax
from jax.experimental import pallas as pl
from jax.experimental.pallas import tpu as pltpu
from jax.sharding import PartitionSpec as P

MESH = pl.DeviceIdType.MESH

TILE = 128
AB = 2
HELD = 3
NS = 48
RING = 8
KA = 8
MINE = HELD * AB
GROUP = RING * MINE
CHUNK = 1
STEP = 8
ROWS = TILE // KA

HOPS = RING // 2
LONGEST = 6


class Plan:
    def __init__(self, sizes, spare):
        self.sizes, self.spare = sizes, spare
        self.zero_slot = GROUP + 2 * sum(sizes)
        self.slots = self.zero_slot + 1
        self.held = sizes[0] + spare[1]
        self.pieces = {1: self.cut(0, sizes[0], "own")}
        self.staged = {}
        self.stage = 0
        for phase in range(2, HOPS + 1):
            size = sizes[phase - 1]
            mixed, back = size - spare[phase - 1], min(size, sizes[0])
            front = self.cut(0, mixed, "front") + self.cut(mixed, back, "mixed")
            rear = self.cut(back, size, "back")
            self.pieces[phase] = rear + front if phase == 2 else front + rear
            self.staged[phase] = self.stage - mixed
            self.stage += back - mixed

    @staticmethod
    def cut(begin, end, kind):
        count = -(-(end - begin) // LONGEST)
        edges = [begin + (end - begin) * i // count for i in range(count + 1)] if count else []
        return [(a, b, kind) for a, b in zip(edges, edges[1:])]

    def region(self, sign, phase):
        return GROUP + sign * sum(self.sizes) + sum(self.sizes[: phase - 1])


USUAL = Plan((22, 24, 22, 12), (0, 12, 9, 6))
EVERY = Plan((GROUP, GROUP, GROUP, GROUP // 2), (0, 0, 0, 0))


def kernel(
    plan, owner_ref, tile_ref, owner_row, tile_row, mask_ref, integrals_ref, amplitude_ref,
    out_ref, flag_ref,
    amp, group, lists, stage, pool, need_tx, need_rx, mask_rx, order, tab_tx, tab_rx, near_tx, near_rx, vote_tx, vote_rx, last_tx, last_rx,
    order_s, tab_s, index_s, total, part_rx,
    local_sem, one_send, one_recv, two_send, two_recv, need_send, need_recv, mask_send, mask_recv,
    tab_send, tab_recv, near_send, near_recv, vote_send, vote_recv, last_send, last_recv, part_send, part_recv,
):
    pair, ka = lax.axis_index("pair"), lax.axis_index("ka")
    core = lax.rem(ka, 2)
    high, low = lax.div(pair, RING), lax.rem(pair, RING)
    u = high + core * (low - high)
    v = low + core * (high - low)
    stride_u, stride_v = RING - (RING - 1) * core, 1 + (RING - 1) * core

    def on_first(step):
        return (lax.rem(u + step + RING, RING) * stride_u + v * stride_v, ka)

    def on_second(step):
        return (u * stride_u + lax.rem(v + step + RING, RING) * stride_v, ka)

    def on_ka(step):
        return (pair, lax.rem(ka + step, KA))

    load_copies = [
        pltpu.make_async_copy(
            integrals_ref.at[:, :, pl.ds(a * TILE, TILE)],
            group.at[pl.ds(u * MINE + a * HELD, HELD)],
            local_sem.at[4 + a],
        )
        for a in range(AB)
    ]
    for copy in load_copies:
        copy.start()

    barrier = pltpu.get_barrier_semaphore()
    for step in range(1, RING):
        for there in (on_first(step), on_second(step), on_ka(step)):
            pl.semaphore_signal(barrier, inc=1, device_id=there, device_id_type=MESH)

    amp_copy = pltpu.make_async_copy(amplitude_ref, amp, local_sem.at[0])

    lane = lax.broadcasted_iota(jnp.int32, (8, TILE), 1)
    own_mask = jnp.zeros((8, TILE), jnp.float32)
    for t in range(HELD):
        for a in range(AB):
            here = lane == u * MINE + a * HELD + t
            own_mask = jnp.where(here, mask_ref[a : a + 1, t : t + 1].astype(jnp.float32), own_mask)
    mask_rx[0] = own_mask

    def source_of(s):
        owner = owner_ref[s]
        oh, ol = lax.div(owner, RING), lax.rem(owner, RING)
        return oh + core * (ol - oh), ol + core * (oh - ol), tile_ref[s]

    slot_lane = lax.broadcasted_iota(jnp.int32, (NS, NS), 1)
    slot_row = lax.broadcasted_iota(jnp.int32, (NS, NS), 0)
    owner_high, owner_low = lax.shift_right_logical(owner_row[...], 3), lax.bitwise_and(owner_row[...], RING - 1)
    owner_u = owner_high + core * (owner_low - owner_high)
    owner_v = owner_low + core * (owner_high - owner_low)
    steps = lax.bitwise_and(owner_v - v, RING - 1)
    target = (steps * TILE + owner_u * MINE + tile_row[...]).astype(jnp.float32)
    target = jnp.sum(jnp.where(slot_lane == slot_row, jnp.broadcast_to(target, (NS, NS)), 0.0), axis=1, keepdims=True)
    ahead = target - lax.broadcasted_iota(jnp.int32, (NS, TILE), 1).astype(jnp.float32)
    for j in range(RING):
        used = jnp.zeros((NS, TILE), jnp.float32)
        for a in range(AB):
            used = jnp.where(ahead == float(j * TILE - a * HELD), 1.0, used)
        need_tx[j] = jnp.broadcast_to(jnp.max(used, axis=0, keepdims=True), (8, TILE))

    pool[plan.zero_slot] = jnp.zeros((TILE, TILE), jnp.bfloat16)

    for copy in load_copies:
        copy.wait()
    pl.semaphore_wait(barrier, 3 * (RING - 1))

    def remote(src, dst, send, recv, there):
        return pltpu.make_async_remote_copy(
            src_ref=src, dst_ref=dst, send_sem=send, recv_sem=recv, device_id=there, device_id_type=MESH
        )

    def first(sign, hop, block, arrival=False):
        behind = lax.rem(u + (hop - 1 + arrival if sign else RING - hop + 1 - arrival), RING)
        ref = group.at[pl.ds(behind * MINE + block, CHUNK)]
        number = (sign * HOPS + hop - 1) * MINE + block
        return remote(ref, ref, one_send.at[number], one_recv.at[number], on_first(-1 if sign else 1))

    def first_wait(sign, hop, block):
        first(sign, hop, block, arrival=True).wait_recv()

    need_copies = [
        remote(need_tx.at[j], need_rx.at[j], need_send.at[j], need_recv.at[j], on_second(j)) for j in range(1, RING)
    ]
    mask_copies = [
        remote(mask_rx.at[0], mask_rx.at[j], mask_send.at[j], mask_recv.at[j], on_first(j)) for j in range(1, RING)
    ]
    sent = []

    def start(copy):
        copy.start()
        sent.append(copy)

    for block in range(0, MINE, CHUNK):
        for sign in range(2):
            start(first(sign, 1, block))
        if block == 0:
            for copy in need_copies + mask_copies:
                start(copy)
    amp_copy.start()

    def forward(hop):
        for block in range(0, MINE, CHUNK):
            for sign in range(2):
                first_wait(sign, hop - 1, block)
                start(first(sign, hop, block))

    forward(2)

    for copy in need_copies + mask_copies:
        copy.wait_recv()
    mask = mask_rx[0]
    for j in range(1, RING):
        mask = jnp.maximum(mask, mask_rx[j])
    even = (lane % 2) == 0
    flane = lane.astype(jnp.float32)
    wide_lane = lax.broadcasted_iota(jnp.int32, (GROUP, TILE), 1)
    wide_row = lax.broadcasted_iota(jnp.int32, (GROUP, TILE), 0)
    far = []
    for sign in range(2):
        reach = jnp.zeros((8, TILE), jnp.float32)
        for distance in range(1, HOPS):
            needed = need_rx[distance if sign else RING - distance] * mask
            reach = jnp.where(needed > 0.0, float(distance), reach)
        far.append(reach)
    opposite = need_rx[HOPS] * mask > 0.0
    far[0] = jnp.where(jnp.logical_and(opposite, even), float(HOPS), far[0])
    far[1] = jnp.where(jnp.logical_and(opposite, jnp.logical_not(even)), float(HOPS), far[1])
    ranks = []
    counts = []
    for sign in range(2):
        counts.append(
            [
                jnp.broadcast_to(
                    jnp.sum(jnp.where(far[sign] >= float(hop), 1.0, 0.0), axis=1, keepdims=True), (8, TILE)
                )
                for hop in range(1, HOPS + 1)
            ]
        )
        key = far[sign] * float(TILE) + (float(TILE - 1) - flane)
        key_row = jnp.broadcast_to(key[0:1], (GROUP, TILE))
        key_col = jnp.sum(jnp.where(wide_lane == wide_row, key_row, 0.0), axis=1, keepdims=True)
        rank_row = jnp.sum(jnp.where(key_col > key_row, 1.0, 0.0), axis=0, keepdims=True)
        rank_col = jnp.sum(jnp.where(key_row > key_col, 1.0, 0.0), axis=1, keepdims=True)
        chosen = jnp.where(rank_col == wide_lane.astype(jnp.float32), wide_row.astype(jnp.float32), 0.0)
        inverse = jnp.sum(chosen, axis=0, keepdims=True)
        order[sign] = jnp.broadcast_to(inverse, (8, TILE)).astype(jnp.int32)
        ranks.append(jnp.broadcast_to(rank_row, (8, TILE)))
    order_copy = pltpu.make_async_copy(order, order_s, local_sem.at[1])
    order_copy.start()
    forward(3)

    sub = lax.broadcasted_iota(jnp.int32, (8, TILE), 0)
    kept = float(plan.sizes[0])

    def slot_of(sign, hops):
        slot = ranks[sign] + float(plan.region(sign, hops))
        if hops < HOPS and plan.spare[hops]:
            last = plan.region(sign, hops + 1) + plan.sizes[hops] - 1
            slot = jnp.where(ranks[sign] >= kept, float(last) + kept - ranks[sign], slot)
        return slot

    rows = jnp.zeros((8, TILE), jnp.float32)
    for sign in range(2):
        for hop in range(2, HOPS + 1):
            rows = jnp.where(sub == sign * (HOPS - 1) + hop - 1, counts[sign][hop - 1], rows)
    for j in range(1, RING):
        if j == HOPS:
            slot = jnp.where(even, slot_of(0, HOPS), slot_of(1, HOPS))
        else:
            slot = slot_of(0, j) if j < HOPS else slot_of(1, RING - j)
        slot = jnp.where(mask > 0.0, slot, float(plan.zero_slot))
        tab_tx[j] = jnp.where(sub == 0, slot, rows).astype(jnp.int32)
    tab_copies = [
        remote(tab_tx.at[j], tab_rx.at[j], tab_send.at[j], tab_recv.at[j], on_second(j)) for j in range(1, RING)
    ]
    tab_rx[0] = jnp.where(mask > 0.0, flane, float(plan.zero_slot)).astype(jnp.int32)

    for copy in tab_copies:
        start(copy)

    for block in range(0, MINE, CHUNK):
        for sign in range(2):
            first_wait(sign, HOPS - 1, block)
            if block * 2 // MINE == sign:
                start(first(sign, HOPS, block))
    order_copy.wait()
    for block in range(0, MINE, CHUNK):
        first_wait(block * 2 // MINE, HOPS, block)

    early = len(sent)

    numbers = {}
    for sign in range(2):
        for phase, pieces in plan.pieces.items():
            for piece in pieces:
                numbers[sign, phase, piece] = len(numbers)

    def second(sign, phase, piece):
        begin, end, kind = piece
        size = end - begin
        if kind == "own":
            src = lists.at[sign, pl.ds(begin, size)]
        elif kind == "front":
            src = pool.at[pl.ds(plan.region(sign, phase - 1) + begin, size)]
        elif kind == "mixed":
            src = stage.at[sign, pl.ds(plan.staged[phase] + begin, size)]
        elif phase == 2:
            src = lists.at[sign, pl.ds(plan.held - plan.sizes[1] + begin, size)]
        else:
            shift = plan.sizes[phase - 2] - plan.sizes[phase - 1]
            src = pool.at[pl.ds(plan.region(sign, phase - 1) + shift + begin, size)]
        number = numbers[sign, phase, piece]
        dst = pool.at[pl.ds(plan.region(sign, phase) + begin, size)]
        return remote(src, dst, two_send.at[number], two_recv.at[number], on_second(-1 if sign else 1))

    arrived = set()

    def await_slots(sign, phase, begin, end):
        for piece in plan.pieces[phase]:
            if piece[0] < end and begin < piece[1] and (sign, phase, piece) not in arrived:
                arrived.add((sign, phase, piece))
                second(sign, phase, piece).wait_recv()

    def pick(sign, place, rank):
        lists[sign, place] = group[jnp.clip(order_s[sign, 0, rank], 0, GROUP - 1)]

    for piece in plan.pieces[1]:
        for sign in range(2):
            for rank in range(piece[0], piece[1]):
                pick(sign, rank, rank)
            start(second(sign, 1, piece))
    for sign in range(2):
        for i in range(plan.spare[1]):
            pick(sign, plan.held - 1 - i, plan.sizes[0] + i)
    for piece in plan.pieces[2]:
        if piece[2] == "back":
            for sign in range(2):
                start(second(sign, 2, piece))
    own_copy = pltpu.make_async_copy(group, pool.at[pl.ds(0, GROUP)], local_sem.at[2])
    own_copy.start()

    for copy in tab_copies:
        copy.wait_recv()
    tab_copy = pltpu.make_async_copy(tab_rx, tab_s, local_sem.at[3])
    tab_copy.start()

    over = jnp.zeros((8, TILE), jnp.float32)
    left_over = {}
    for sign in range(2):
        moving = [counts[sign][0]]
        for behind in range(1, HOPS):
            table = tab_rx[RING - behind if sign else behind].astype(jnp.float32)
            for hop in (behind, behind + 1):
                if hop > 1:
                    row = sign * (HOPS - 1) + hop - 1
                    moving.append(jnp.broadcast_to(table[row : row + 1], (8, TILE)))
        passed = {2: moving[1], 3: moving[3], 4: moving[5]}
        came = {2: moving[0], 3: moving[1], 4: moving[3]}
        over = jnp.maximum(over, jnp.where(passed[HOPS] > kept, 1.0, 0.0))
        for phase in range(2, HOPS + 1):
            rest = jnp.maximum(came[phase] - kept, 0.0)
            front = jnp.minimum(passed[phase], kept)
            over = jnp.maximum(over, jnp.where(rest > float(plan.spare[phase - 1]), 1.0, 0.0))
            over = jnp.maximum(over, jnp.where(rest + front > float(plan.sizes[phase - 1]), 1.0, 0.0))
            left_over[sign, phase] = rest

    def spread(vote, tx, rx, send, recv, there):
        tx[...] = vote
        copies = [remote(tx, rx.at[j], send.at[j], recv.at[j], there(j)) for j in range(1, RING)]
        for copy in copies:
            start(copy)
        return copies

    def collect(copies, tx, rx):
        for copy in copies:
            copy.wait_recv()
        vote = tx[...]
        for j in range(1, RING):
            vote = jnp.maximum(vote, rx[j])
        return vote

    near_copies = spread(over, near_tx, near_rx, near_send, near_recv, on_second)

    tab_copy.wait()

    def locate(s, carry):
        su, sv, st = source_of(s)
        distance = lax.rem(v - sv + RING, RING)
        for a in range(AB):
            slot = tab_s[distance, 0, su * MINE + a * HELD + st]
            index_s[s * AB + a] = jnp.clip(slot, 0, plan.zero_slot)
        return carry

    lax.fori_loop(0, NS, locate, 0)

    for copy in sent[:early]:
        copy.wait_send()
    del sent[:early]
    for phase in range(2, HOPS + 1):
        size, shift = plan.sizes[phase - 1], plan.sizes[phase - 2] - plan.sizes[phase - 1]
        behind = len(sent)
        for piece in plan.pieces[phase]:
            begin, end, kind = piece
            if phase == 2 and kind == "back":
                continue
            for sign in range(2):
                before = plan.region(sign, phase - 1)
                if kind == "back":
                    await_slots(sign, phase - 1, begin + shift, end + shift)
                else:
                    await_slots(sign, phase - 1, begin, end)
                if kind == "mixed":
                    if phase > 2:
                        await_slots(sign, phase - 1, begin + shift, end + shift)
                    for slot in range(begin, end):
                        if phase > 2:
                            other = pool[before + slot + shift]
                        else:
                            other = lists[sign, plan.held - size + slot]
                        rest = jnp.broadcast_to(left_over[sign, phase][0:1], (TILE, TILE))
                        chosen = jnp.where(
                            rest > float(size - 1 - slot), other.astype(jnp.float32), pool[before + slot].astype(jnp.float32)
                        )
                        stage[sign, plan.staged[phase] + slot] = chosen.astype(jnp.bfloat16)
                start(second(sign, phase, piece))
        if phase == 2:
            vote = collect(near_copies, near_tx, near_rx)
            vote_copies = spread(vote, vote_tx, vote_rx, vote_send, vote_recv, on_first)
        elif phase == 3:
            vote = collect(vote_copies, vote_tx, vote_rx)
            last_copies = spread(vote, last_tx, last_rx, last_send, last_recv, on_ka)
    flag_ref[0] = jnp.max(collect(last_copies, last_tx, last_rx)).astype(jnp.int32)
    for copy in sent[:behind]:
        copy.wait_send()
    del sent[:behind]
    own_copy.wait()
    amp_copy.wait()
    for phase in range(1, HOPS + 1):
        for sign in range(2):
            await_slots(sign, phase, 0, plan.sizes[phase - 1])

    total[...] = jnp.zeros_like(total)

    def multiply(i, carry):
        tiles = [amp[STEP * i + j] for j in range(STEP)]
        bands = [
            jnp.concatenate([pool[index_s[(STEP * i + j) * AB + a]] for j in range(STEP)], axis=0) for a in range(AB)
        ]
        total[...] += jnp.dot(
            jnp.concatenate(tiles, axis=1), jnp.concatenate(bands, axis=1), preferred_element_type=jnp.float32
        )
        return carry

    lax.fori_loop(0, NS // STEP, multiply, 0)

    part_copies = [
        remote(
            total.at[pl.ds(lax.rem(ka + j, KA) * ROWS, ROWS)], part_rx.at[j], part_send.at[j], part_recv.at[j], on_ka(j)
        )
        for j in range(1, KA)
    ]
    for copy in part_copies:
        copy.start()
    for copy in sent:
        copy.wait_send()
    result = total[pl.ds(pl.multiple_of(ka * ROWS, ROWS), ROWS)]
    for j, copy in enumerate(part_copies, 1):
        copy.wait_recv()
        result += part_rx[j]
    out_ref[...] = result
    for copy in part_copies:
        copy.wait_send()


def ladder(plan, number, amplitude, slot_owner, slot_tile, integrals, tile_mask):
    copies = 2 * sum(len(pieces) for pieces in plan.pieces.values())
    scratch = [
        pltpu.VMEM((NS, TILE, TILE), jnp.bfloat16),
        pltpu.VMEM((GROUP, TILE, TILE), jnp.bfloat16),
        pltpu.VMEM((2, plan.held, TILE, TILE), jnp.bfloat16),
        pltpu.VMEM((2, max(plan.stage, 1), TILE, TILE), jnp.bfloat16),
        pltpu.VMEM((plan.slots, TILE, TILE), jnp.bfloat16),
        pltpu.VMEM((RING, 8, TILE), jnp.float32),
        pltpu.VMEM((RING, 8, TILE), jnp.float32),
        pltpu.VMEM((RING, 8, TILE), jnp.float32),
        pltpu.VMEM((2, 8, TILE), jnp.int32),
        pltpu.VMEM((RING, 8, TILE), jnp.int32),
        pltpu.VMEM((RING, 8, TILE), jnp.int32),
        pltpu.VMEM((8, TILE), jnp.float32),
        pltpu.VMEM((RING, 8, TILE), jnp.float32),
        pltpu.VMEM((8, TILE), jnp.float32),
        pltpu.VMEM((RING, 8, TILE), jnp.float32),
        pltpu.VMEM((8, TILE), jnp.float32),
        pltpu.VMEM((KA, 8, TILE), jnp.float32),
        pltpu.SMEM((2, 8, TILE), jnp.int32),
        pltpu.SMEM((RING, 8, TILE), jnp.int32),
        pltpu.SMEM((NS * AB,), jnp.int32),
        pltpu.VMEM((TILE, AB * TILE), jnp.float32),
        pltpu.VMEM((KA, ROWS, AB * TILE), jnp.float32),
        pltpu.SemaphoreType.DMA((6,)),
        pltpu.SemaphoreType.DMA((2 * HOPS * MINE,)),
        pltpu.SemaphoreType.DMA((2 * HOPS * MINE,)),
        pltpu.SemaphoreType.DMA((copies,)),
        pltpu.SemaphoreType.DMA((copies,)),
    ] + [pltpu.SemaphoreType.DMA((RING,)) for _ in range(14)]
    smem, vmem = pl.BlockSpec(memory_space=pltpu.SMEM), pl.BlockSpec(memory_space=pltpu.VMEM)
    hbm = pl.BlockSpec(memory_space=pl.ANY)
    return pl.pallas_call(
        functools.partial(kernel, plan),
        out_shape=(
            jax.ShapeDtypeStruct((ROWS, AB * TILE), jnp.float32),
            jax.ShapeDtypeStruct((1,), jnp.int32),
        ),
        in_specs=[smem, smem, vmem, vmem, vmem, hbm, hbm],
        out_specs=(vmem, smem),
        scratch_shapes=scratch,
        compiler_params=pltpu.CompilerParams(
            collective_id=number, has_side_effects=True, vmem_limit_bytes=32 * 1024 * 1024
        ),
    )(slot_owner, slot_tile, slot_owner[None], slot_tile[None], tile_mask.T, integrals, amplitude)


def local(*arrays):
    result, over = ladder(USUAL, 0, *arrays)
    return lax.cond(over[0] > 0, lambda: ladder(EVERY, 1, *arrays)[0], lambda: result)


def solution(mesh):
    in_specs = (
        P(("pair", "ka"), None, None),
        P(("pair", "ka")),
        P(("pair", "ka")),
        P(("pair", "ka"), None, None),
        P(("pair", "ka"), None),
    )
    out_specs = P(("pair", "ka"), None)
    return jax.shard_map(local, mesh=mesh, in_specs=in_specs, out_specs=out_specs, check_vma=False)
```

time: 77.5 us -> 73.8 us (0.952)
  Pallas kernels: 76 us -> 72.3 us
    pallas_call x1, Pallas kernels: 76 us -> 72.3 us  [ladder(): pl.pallas_call(functools.partial(kernel, plan), out_shape=(jax.ShapeDtype...]
where the time goes in v4:
time: 73.8 us; the launch traced here: 73.7 us
  Pallas kernels  72.3 us (98%)
  between operations  0.76 us (1%)
    pallas_call x1, Pallas kernels, ladder(): pl.pallas_call(functools.partial(kernel, plan), out_shape=(jax.ShapeDtype...  72.3 us

profile of v4, /device:TPU:1, one launch (start us, length us, event | category | flops | bytes accessed | tf_op | source)
XLA Modules:
  0.0 73.7 jit_solution(15613102708262787898)
XLA Ops:
  0.0 0.0 copy-start.3
  0.0 0.0 copy-start.2
  0.0 0.0 copy-start.4
  0.0 0.0 copy-start.1
  0.0 0.0 copy-start
  0.0 72.3 %shard_map.57 = (f32[16,256]{1,0:T(8,128)S(1)}, s32[1]{0:T(128)}) custom-call(s32[48]{0:T(128)} %owner_ref.1, s32[48]{0:T(128)} %tile_ref.1, s32[1,48]{1,0:T(1,128)} %bitcast.7, s32[1,48]{1,0:T(1,128)} %bitcast.9, s32[2,3]{1,0:T(2,128)} %bitcast.11, bf16[3,128,256]{2,1,0:T(8,128)(2,1)} %integrals_ref.1, bf16[48,128,128]{2,1,0:T(8,128)(2,1)} %amplitude_ref.1), custom_call_target="tpu_custom_call" | custom-call | tf_op jit(solution)/shard_map/pallas_call | solution.py:477
  73.0 0.0 copy-done.3
  73.0 0.0 copy-done.2
  73.0 0.0 copy-done.4
  73.0 0.0 copy-done.1
  73.1 0.0 copy-done
  73.1 0.6 copy.11
  (1 shorter events, 0.0 us)
Async XLA Ops:
  0.0 73.0 %copy-start.3 = (s32[48]{0:T(128)S(1)}, s32[48]{0:T(128)}, u32[]{:S(2)}) copy-start(s32[48]{0:T(128)} %tile_ref.1) | copy-start | bytes 580
  0.0 73.0 %copy-start.2 = (s32[48]{0:T(128)S(1)}, s32[48]{0:T(128)}, u32[]{:S(2)}) copy-start(s32[48]{0:T(128)} %owner_ref.1) | copy-start | bytes 580
  0.0 73.0 %copy-start.4 = (s32[3,2]{0,1:T(2,128)S(1)}, s32[3,2]{0,1:T(2,128)}, u32[]{:S(2)}) copy-start(s32[3,2]{0,1:T(2,128)} %param.11) | copy-start | bytes 76
  0.0 73.0 %copy-start.1 = (bf16[3,128,256]{2,1,0:T(8,128)(2,1)S(1)}, bf16[3,128,256]{2,1,0:T(8,128)(2,1)}, u32[]{:S(2)}) copy-start(bf16[3,128,256]{2,1,0:T(8,128)(2,1)} %integrals_ref.1) | copy-start | bytes 589828
  0.0 73.0 %copy-start = (bf16[48,128,128]{2,1,0:T(8,128)(2,1)S(1)}, bf16[48,128,128]{2,1,0:T(8,128)(2,1)}, u32[]{:S(2)}) copy-start(bf16[48,128,128]{2,1,0:T(8,128)(2,1)} %amplitude_ref.1) | copy-start | bytes 4718596

commit v5 on v4

--- a/solution.py
+++ b/solution.py
@@ -22,7 +22,7 @@
 ROWS = TILE // KA
 
 HOPS = RING // 2
-LONGEST = 6
+LONGEST = 4
 
 
 class Plan:
@@ -58,9 +58,9 @@
 
 
 def kernel(
-    plan, owner_ref, tile_ref, owner_row, tile_row, mask_ref, integrals_ref, amplitude_ref,
+    plan, owner_hbm, tile_hbm, owner_row_hbm, tile_row_hbm, mask_hbm, integrals_ref, amplitude_ref,
     out_ref, flag_ref,
-    amp, group, lists, stage, pool, need_tx, need_rx, mask_rx, order, tab_tx, tab_rx, near_tx, near_rx, vote_tx, vote_rx, last_tx, last_rx,
+    owner_ref, tile_ref, owner_row, tile_row, mask_ref, amp, group, lists, stage, pool, need_tx, need_rx, mask_rx, order, tab_tx, tab_rx, near_tx, near_rx, vote_tx, vote_rx, last_tx, last_rx,
     order_s, tab_s, index_s, total, part_rx,
     local_sem, one_send, one_recv, two_send, two_recv, need_send, need_recv, mask_send, mask_recv,
     tab_send, tab_recv, near_send, near_recv, vote_send, vote_recv, last_send, last_recv, part_send, part_recv,
@@ -92,6 +92,21 @@
     for copy in load_copies:
         copy.start()
 
+    small_copies = [
+        pltpu.make_async_copy(source, target, local_sem.at[6 + i])
+        for i, (source, target) in enumerate(
+            (
+                (owner_row_hbm, owner_row),
+                (tile_row_hbm, tile_row),
+                (mask_hbm, mask_ref),
+                (owner_hbm, owner_ref),
+                (tile_hbm, tile_ref),
+            )
+        )
+    ]
+    for copy in small_copies:
+        copy.start()
+
     barrier = pltpu.get_barrier_semaphore()
     for step in range(1, RING):
         for there in (on_first(step), on_second(step), on_ka(step)):
@@ -99,6 +114,8 @@
 
     amp_copy = pltpu.make_async_copy(amplitude_ref, amp, local_sem.at[0])
 
+    for copy in small_copies:
+        copy.wait()
     lane = lax.broadcasted_iota(jnp.int32, (8, TILE), 1)
     own_mask = jnp.zeros((8, TILE), jnp.float32)
     for t in range(HELD):
@@ -162,7 +179,7 @@
     for block in range(0, MINE, CHUNK):
         for sign in range(2):
             start(first(sign, 1, block))
-        if block == 0:
+        if block == HELD - CHUNK:
             for copy in need_copies + mask_copies:
                 start(copy)
     amp_copy.start()
@@ -444,6 +461,11 @@
 def ladder(plan, number, amplitude, slot_owner, slot_tile, integrals, tile_mask):
     copies = 2 * sum(len(pieces) for pieces in plan.pieces.values())
     scratch = [
+        pltpu.SMEM((NS,), jnp.int32),
+        pltpu.SMEM((NS,), jnp.int32),
+        pltpu.VMEM((1, NS), jnp.int32),
+        pltpu.VMEM((1, NS), jnp.int32),
+        pltpu.VMEM((AB, HELD), jnp.int32),
         pltpu.VMEM((NS, TILE, TILE), jnp.bfloat16),
         pltpu.VMEM((GROUP, TILE, TILE), jnp.bfloat16),
         pltpu.VMEM((2, plan.held, TILE, TILE), jnp.bfloat16),
@@ -466,7 +488,7 @@
         pltpu.SMEM((NS * AB,), jnp.int32),
         pltpu.VMEM((TILE, AB * TILE), jnp.float32),
         pltpu.VMEM((KA, ROWS, AB * TILE), jnp.float32),
-        pltpu.SemaphoreType.DMA((6,)),
+        pltpu.SemaphoreType.DMA((11,)),
         pltpu.SemaphoreType.DMA((2 * HOPS * MINE,)),
         pltpu.SemaphoreType.DMA((2 * HOPS * MINE,)),
         pltpu.SemaphoreType.DMA((copies,)),
@@ -480,7 +502,7 @@
             jax.ShapeDtypeStruct((ROWS, AB * TILE), jnp.float32),
             jax.ShapeDtypeStruct((1,), jnp.int32),
         ),
-        in_specs=[smem, smem, vmem, vmem, vmem, hbm, hbm],
+        in_specs=[hbm] * 7,
         out_specs=(vmem, smem),
         scratch_shapes=scratch,
         compiler_params=pltpu.CompilerParams(

time: 73.8 us -> 72.4 us (0.981)
  Pallas kernels: 72.3 us -> 70.9 us
    pallas_call x1, Pallas kernels: 72.3 us -> 70.9 us  [ladder(): pl.pallas_call(functools.partial(kernel, plan), out_shape=(jax.ShapeDtype...]
where the time goes in v5:
time: 72.4 us; the launch traced here: 72.3 us
  Pallas kernels  70.9 us (98%)
  between operations  0.76 us (1%)
    pallas_call x1, Pallas kernels, ladder(): pl.pallas_call(functools.partial(kernel, plan), out_shape=(jax.ShapeDtype...  70.9 us

profile of v5, /device:TPU:1, one launch (start us, length us, event | category | flops | bytes accessed | tf_op | source)
XLA Modules:
  0.0 72.3 jit_solution(17011134993570316393)
XLA Ops:
  0.0 0.0 copy-start.3
  0.0 0.0 copy-start.2
  0.0 0.0 copy-start.4
  0.0 0.0 copy-start.1
  0.0 0.0 copy-start
  0.0 70.9 %shard_map.57 = (f32[16,256]{1,0:T(8,128)S(1)}, s32[1]{0:T(128)}) custom-call(s32[48]{0:T(128)} %owner_hbm.1, s32[48]{0:T(128)} %tile_hbm.1, s32[1,48]{1,0:T(1,128)} %bitcast.7, s32[1,48]{1,0:T(1,128)} %bitcast.9, s32[2,3]{1,0:T(2,128)} %bitcast.11, bf16[3,128,256]{2,1,0:T(8,128)(2,1)} %integrals_ref.1, bf16[48,128,128]{2,1,0:T(8,128)(2,1)} %amplitude_ref.1), custom_call_target="tpu_custom_call" | custom-call | tf_op jit(solution)/shard_map/pallas_call | solution.py:499
  71.6 0.0 copy-done.3
  71.6 0.0 copy-done.2
  71.6 0.0 copy-done.4
  71.6 0.0 copy-done.1
  71.6 0.0 copy-done
  71.7 0.6 copy.11
  (1 shorter events, 0.0 us)
Async XLA Ops:
  0.0 71.6 %copy-start.3 = (s32[48]{0:T(128)S(1)}, s32[48]{0:T(128)}, u32[]{:S(2)}) copy-start(s32[48]{0:T(128)} %tile_hbm.1) | copy-start | bytes 580
  0.0 71.6 %copy-start.2 = (s32[48]{0:T(128)S(1)}, s32[48]{0:T(128)}, u32[]{:S(2)}) copy-start(s32[48]{0:T(128)} %owner_hbm.1) | copy-start | bytes 580
  0.0 71.6 %copy-start.4 = (s32[3,2]{0,1:T(2,128)S(1)}, s32[3,2]{0,1:T(2,128)}, u32[]{:S(2)}) copy-start(s32[3,2]{0,1:T(2,128)} %param.11) | copy-start | bytes 76
  0.0 71.6 %copy-start.1 = (bf16[3,128,256]{2,1,0:T(8,128)(2,1)S(1)}, bf16[3,128,256]{2,1,0:T(8,128)(2,1)}, u32[]{:S(2)}) copy-start(bf16[3,128,256]{2,1,0:T(8,128)(2,1)} %integrals_ref.1) | copy-start | bytes 589828
  0.0 71.6 %copy-start = (bf16[48,128,128]{2,1,0:T(8,128)(2,1)S(1)}, bf16[48,128,128]{2,1,0:T(8,128)(2,1)}, u32[]{:S(2)}) copy-start(bf16[48,128,128]{2,1,0:T(8,128)(2,1)} %amplitude_ref.1) | copy-start | bytes 4718596

commit v6 on v5

--- a/solution.py
+++ b/solution.py
@@ -53,7 +53,7 @@
         return GROUP + sign * sum(self.sizes) + sum(self.sizes[: phase - 1])
 
 
-USUAL = Plan((22, 24, 22, 12), (0, 12, 9, 6))
+USUAL = Plan((22, 24, 22, 12), (0, 12, 11, 6))
 EVERY = Plan((GROUP, GROUP, GROUP, GROUP // 2), (0, 0, 0, 0))
 
 
@@ -104,15 +104,48 @@
             )
         )
     ]
-    for copy in small_copies:
-        copy.start()
-
     barrier = pltpu.get_barrier_semaphore()
     for step in range(1, RING):
         for there in (on_first(step), on_second(step), on_ka(step)):
             pl.semaphore_signal(barrier, inc=1, device_id=there, device_id_type=MESH)
 
+    for copy in small_copies:
+        copy.start()
     amp_copy = pltpu.make_async_copy(amplitude_ref, amp, local_sem.at[0])
+
+    for copy in load_copies:
+        copy.wait()
+    pl.semaphore_wait(barrier, 3 * (RING - 1))
+
+    def remote(src, dst, send, recv, there):
+        return pltpu.make_async_remote_copy(
+            src_ref=src, dst_ref=dst, send_sem=send, recv_sem=recv, device_id=there, device_id_type=MESH
+        )
+
+    def first(sign, hop, block, arrival=False):
+        behind = lax.rem(u + (hop - 1 + arrival if sign else RING - hop + 1 - arrival), RING)
+        ref = group.at[pl.ds(behind * MINE + block, CHUNK)]
+        number = (sign * HOPS + hop - 1) * MINE + block
+        return remote(ref, ref, one_send.at[number], one_recv.at[number], on_first(-1 if sign else 1))
+
+    def first_wait(sign, hop, block):
+        first(sign, hop, block, arrival=True).wait_recv()
+
+    need_copies = [
+        remote(need_tx.at[j], need_rx.at[j], need_send.at[j], need_recv.at[j], on_second(j)) for j in range(1, RING)
+    ]
+    mask_copies = [
+        remote(mask_rx.at[0], mask_rx.at[j], mask_send.at[j], mask_recv.at[j], on_first(j)) for j in range(1, RING)
+    ]
+    sent = []
+
+    def start(copy):
+        copy.start()
+        sent.append(copy)
+
+    for block in range(0, MINE, CHUNK):
+        for sign in range(2):
+            start(first(sign, 1, block))
 
     for copy in small_copies:
         copy.wait()
@@ -123,11 +156,6 @@
             here = lane == u * MINE + a * HELD + t
             own_mask = jnp.where(here, mask_ref[a : a + 1, t : t + 1].astype(jnp.float32), own_mask)
     mask_rx[0] = own_mask
-
-    def source_of(s):
-        owner = owner_ref[s]
-        oh, ol = lax.div(owner, RING), lax.rem(owner, RING)
-        return oh + core * (ol - oh), ol + core * (oh - ol), tile_ref[s]
 
     slot_lane = lax.broadcasted_iota(jnp.int32, (NS, NS), 1)
     slot_row = lax.broadcasted_iota(jnp.int32, (NS, NS), 0)
@@ -143,46 +171,15 @@
         for a in range(AB):
             used = jnp.where(ahead == float(j * TILE - a * HELD), 1.0, used)
         need_tx[j] = jnp.broadcast_to(jnp.max(used, axis=0, keepdims=True), (8, TILE))
-
+    for copy in need_copies + mask_copies:
+        start(copy)
+    amp_copy.start()
     pool[plan.zero_slot] = jnp.zeros((TILE, TILE), jnp.bfloat16)
 
-    for copy in load_copies:
-        copy.wait()
-    pl.semaphore_wait(barrier, 3 * (RING - 1))
-
-    def remote(src, dst, send, recv, there):
-        return pltpu.make_async_remote_copy(
-            src_ref=src, dst_ref=dst, send_sem=send, recv_sem=recv, device_id=there, device_id_type=MESH
-        )
-
-    def first(sign, hop, block, arrival=False):
-        behind = lax.rem(u + (hop - 1 + arrival if sign else RING - hop + 1 - arrival), RING)
-        ref = group.at[pl.ds(behind * MINE + block, CHUNK)]
-        number = (sign * HOPS + hop - 1) * MINE + block
-        return remote(ref, ref, one_send.at[number], one_recv.at[number], on_first(-1 if sign else 1))
-
-    def first_wait(sign, hop, block):
-        first(sign, hop, block, arrival=True).wait_recv()
-
-    need_copies = [
-        remote(need_tx.at[j], need_rx.at[j], need_send.at[j], need_recv.at[j], on_second(j)) for j in range(1, RING)
-    ]
-    mask_copies = [
-        remote(mask_rx.at[0], mask_rx.at[j], mask_send.at[j], mask_recv.at[j], on_first(j)) for j in range(1, RING)
-    ]
-    sent = []
-
-    def start(copy):
-        copy.start()
-        sent.append(copy)
-
-    for block in range(0, MINE, CHUNK):
-        for sign in range(2):
-            start(first(sign, 1, block))
-        if block == HELD - CHUNK:
-            for copy in need_copies + mask_copies:
-                start(copy)
-    amp_copy.start()
+    def source_of(s):
+        owner = owner_ref[s]
+        oh, ol = lax.div(owner, RING), lax.rem(owner, RING)
+        return oh + core * (ol - oh), ol + core * (oh - ol), tile_ref[s]
 
     def forward(hop):
         for block in range(0, MINE, CHUNK):
@@ -191,6 +188,7 @@
                 start(first(sign, hop, block))
 
     forward(2)
+    forward(3)
 
     for copy in need_copies + mask_copies:
         copy.wait_recv()
@@ -233,7 +231,6 @@
         ranks.append(jnp.broadcast_to(rank_row, (8, TILE)))
     order_copy = pltpu.make_async_copy(order, order_s, local_sem.at[1])
     order_copy.start()
-    forward(3)
 
     sub = lax.broadcasted_iota(jnp.int32, (8, TILE), 0)
     kept = float(plan.sizes[0])

time: 72.4 us -> 73.2 us (1.011)
    pallas_call x1, Pallas kernels: 70.9 us -> 71.6 us  [ladder(): pl.pallas_call(functools.partial(kernel, plan), out_shape=(jax.ShapeDtype...]
where the time goes in v6:
time: 73.2 us; the launch traced here: 73 us
  Pallas kernels  71.6 us (98%)
  between operations  0.76 us (1%)
    pallas_call x1, Pallas kernels, ladder(): pl.pallas_call(functools.partial(kernel, plan), out_shape=(jax.ShapeDtype...  71.6 us

profile of v6, /device:TPU:1, one launch (start us, length us, event | category | flops | bytes accessed | tf_op | source)
XLA Modules:
  0.0 73.0 jit_solution(11902685536273089236)
XLA Ops:
  0.0 0.0 copy-start.3
  0.0 0.0 copy-start.2
  0.0 0.0 copy-start.4
  0.0 0.0 copy-start.1
  0.0 0.0 copy-start
  0.0 71.6 %shard_map.57 = (f32[16,256]{1,0:T(8,128)S(1)}, s32[1]{0:T(128)}) custom-call(s32[48]{0:T(128)} %owner_hbm.1, s32[48]{0:T(128)} %tile_hbm.1, s32[1,48]{1,0:T(1,128)} %bitcast.7, s32[1,48]{1,0:T(1,128)} %bitcast.9, s32[2,3]{1,0:T(2,128)} %bitcast.11, bf16[3,128,256]{2,1,0:T(8,128)(2,1)} %integrals_ref.1, bf16[48,128,128]{2,1,0:T(8,128)(2,1)} %amplitude_ref.1), custom_call_target="tpu_custom_call" | custom-call | tf_op jit(solution)/shard_map/pallas_call | solution.py:496
  72.4 0.0 copy-done.3
  72.4 0.0 copy-done.2
  72.4 0.0 copy-done.4
  72.4 0.0 copy-done.1
  72.4 0.0 copy-done
  72.4 0.6 copy.11
  (1 shorter events, 0.0 us)
Async XLA Ops:
  0.0 72.4 %copy-start.3 = (s32[48]{0:T(128)S(1)}, s32[48]{0:T(128)}, u32[]{:S(2)}) copy-start(s32[48]{0:T(128)} %tile_hbm.1) | copy-start | bytes 580
  0.0 72.4 %copy-start.2 = (s32[48]{0:T(128)S(1)}, s32[48]{0:T(128)}, u32[]{:S(2)}) copy-start(s32[48]{0:T(128)} %owner_hbm.1) | copy-start | bytes 580
  0.0 72.4 %copy-start.4 = (s32[3,2]{0,1:T(2,128)S(1)}, s32[3,2]{0,1:T(2,128)}, u32[]{:S(2)}) copy-start(s32[3,2]{0,1:T(2,128)} %param.11) | copy-start | bytes 76
  0.0 72.4 %copy-start.1 = (bf16[3,128,256]{2,1,0:T(8,128)(2,1)S(1)}, bf16[3,128,256]{2,1,0:T(8,128)(2,1)}, u32[]{:S(2)}) copy-start(bf16[3,128,256]{2,1,0:T(8,128)(2,1)} %integrals_ref.1) | copy-start | bytes 589828
  0.0 72.4 %copy-start = (bf16[48,128,128]{2,1,0:T(8,128)(2,1)S(1)}, bf16[48,128,128]{2,1,0:T(8,128)(2,1)}, u32[]{:S(2)}) copy-start(bf16[48,128,128]{2,1,0:T(8,128)(2,1)} %amplitude_ref.1) | copy-start | bytes 4718596
